TPU v7x, 32 devices: a whole 2x2x4 slice. The times are simulated.
32 devices in a mesh: clips: 8 (over y, x, core), tm: 4 (over z).
Axes of the slice: x: 2, y: 2, z: 4, core: 2. Of those that a mesh axis runs over, the one named last changes fastest.
Arguments:
- patches: bfloat16 [64, 512, 768], P('clips', 'tm'), may hold values from -6 to 6
- mask_index: int32 [64, 450], P('clips'), may hold values from 0 to 511, as said below
- mask_count: int32 [64], P('clips'), may hold values from 100 to 450, as said below
- w_qkv: bfloat16 [768, 2304], replicated, may hold values from -0.21875 to 0.21875
- q_bias: bfloat16 [768], replicated, may hold values from -3 to 3
- v_bias: bfloat16 [768], replicated, may hold values from -3 to 3
- w_out: bfloat16 [768, 768], replicated, may hold values from -0.875 to 0.875
- out_bias: bfloat16 [768], replicated, may hold values from -3 to 3
- w_up: bfloat16 [768, 3072], replicated, may hold values from -0.21875 to 0.21875
- up_bias: bfloat16 [3072], replicated, may hold values from -3 to 3
- w_down: bfloat16 [3072, 768], replicated, may hold values from -0.109375 to 0.109375
- down_bias: bfloat16 [768], replicated, may hold values from -3 to 3
- norm1_scale: bfloat16 [768], replicated, may hold values from 0.5 to 1.5
- norm1_shift: bfloat16 [768], replicated, may hold values from -3 to 3
- norm2_scale: bfloat16 [768], replicated, may hold values from 0.5 to 1.5
- norm2_shift: bfloat16 [768], replicated, may hold values from -3 to 3
- mask_embed: bfloat16 [768], replicated, may hold values from -6 to 6
- pos_embed: bfloat16 [512, 768], replicated, may hold values from -3 to 3
- cotangent: bfloat16 [64, 512, 768], P('clips', 'tm'), may hold values from -6 to 6
Outputs:
- block_out: bfloat16 [64, 512, 768], P('clips', 'tm')
- input_grad: bfloat16 [64, 512, 768], P('clips', 'tm')
- grad_w_qkv: float32 [768, 2304], replicated
- grad_q_bias: float32 [768], replicated
- grad_v_bias: float32 [768], replicated
- grad_w_out: float32 [768, 768], replicated
- grad_out_bias: float32 [768], replicated
- grad_w_up: float32 [768, 3072], replicated
- grad_up_bias: float32 [3072], replicated
- grad_w_down: float32 [3072, 768], replicated
- grad_down_bias: float32 [768], replicated
- grad_norm1_scale: float32 [768], replicated
- grad_norm1_shift: float32 [768], replicated
- grad_norm2_scale: float32 [768], replicated
- grad_norm2_shift: float32 [768], replicated
- grad_mask_embed: float32 [768], replicated
- grad_pos_embed: float32 [512, 768], replicated
Inputs may be any that keep to these rules, and one draw needn't show every extreme that they name: `mask_index`: the entries of one clip's list are distinct positions of that clip; the entries after its first mask_count ones are other positions and are not masked. `mask_count`: every draw has a clip with exactly 450 and a clip with exactly 100 masked positions.
All inputs are finite; a program needn't handle non-finite values.
Results may differ from a plain program's by a relative error of at most 0.012.
Values may be sent and summed in bfloat16 or wider, within the bound.
No kernel may reach another device: no remote copies, remote signals or barrier semaphores. Data moves between devices by JAX's collectives and lax.ppermute only.
A program may use at most 256 MiB of HBM per device.

v0:
```python
import functools

import jax
import jax.numpy as jnp
from jax import lax
from jax.experimental import pallas as pl
from jax.experimental.pallas import tpu as pltpu
from jax.sharding import PartitionSpec as P

HEADS = 12
LANES = 128
NORM_EPS = 1e-06
ROOT_HALF = 0.7071067811865476
ROOT_TWO_PI = 2.5066282746310002
LOG2_E = 1.4426950408889634
F32 = jnp.float32
BF16 = jnp.bfloat16
VMEM_LIMIT = 60 * 2**20


def contract(a, b, da, db):
    return lax.dot_general(a, b, (((da,), (db,)), ((), ())), preferred_element_type=F32)


def call(kernel, *, grid, in_specs, out_specs, out_shape, scratch=(), prefetch=0, flops=0, moved=0, exps=0, share=1):
    return pl.pallas_call(
        kernel,
        grid_spec=pltpu.PrefetchScalarGridSpec(
            num_scalar_prefetch=prefetch,
            grid=grid,
            in_specs=in_specs,
            out_specs=out_specs,
            scratch_shapes=scratch,
        ),
        out_shape=out_shape,
        cost_estimate=pl.CostEstimate(
            flops=int(flops) // share, bytes_accessed=int(moved) // share, transcendentals=int(exps) // share
        ),
        compiler_params=pltpu.CompilerParams(vmem_limit_bytes=VMEM_LIMIT),
    )


def fixed(shape):
    return pl.BlockSpec(shape, lambda *_: (0,) * len(shape), pipeline_mode=pl.Buffered(1))


def shaped(shape, dtype):
    return jax.ShapeDtypeStruct(shape, dtype)


def norm_parts(values):
    centred = values - jnp.mean(values, -1, keepdims=True)
    spread = jnp.mean(centred * centred, -1, keepdims=True)
    inverse = lax.rsqrt(spread + NORM_EPS)
    return centred * inverse, inverse


def norm_backward(grad_norm, unit, inverse, gains):
    scaled = grad_norm * gains
    return inverse * (
        scaled
        - jnp.mean(scaled, -1, keepdims=True)
        - unit * jnp.mean(scaled * unit, -1, keepdims=True)
    )


def project_kernel(*refs, tm):
    blocks = refs[:tm]
    mask_ref, embed_ref, pos_ref, gain_ref, shift_ref, w_ref, bias_ref, filled_ref, turned_ref, joint_ref, normed_s = refs[tm:]

    @pl.when(pl.program_id(0) == 0)
    def _():
        seg = blocks[0].shape[0]
        embed, gain, shift = (r[...].astype(F32) for r in (embed_ref, gain_ref, shift_ref))
        for d in range(tm):
            rows = slice(d * seg, (d + 1) * seg)
            filled = jnp.where(mask_ref[rows] > 0.5, embed, blocks[d][...].astype(F32)) + pos_ref[rows].astype(F32)
            unit, _ = norm_parts(filled)
            normed = (unit * gain + shift).astype(BF16)
            filled_ref[rows] = filled
            normed_s[rows] = normed
            turned_ref[:, rows] = normed.T

    joint_ref[...] = (contract(normed_s[...], w_ref[...], 1, 0) + bias_ref[...].astype(F32)).astype(BF16)


def project(blocks, mask, embed, pos, gain, shift, w_qkv, bias):
    tm = len(blocks)
    seg, width = blocks[0].shape
    rows = tm * seg
    return call(
        functools.partial(project_kernel, tm=tm),
        grid=(3,),
        in_specs=[fixed((seg, width))] * tm
        + [fixed((rows, 1)), fixed((1, width)), fixed((rows, width)), fixed((1, width)), fixed((1, width))]
        + [pl.BlockSpec((width, width), lambda j: (0, j)), pl.BlockSpec((1, width), lambda j: (0, j))],
        out_specs=[
            pl.BlockSpec((rows, width), lambda j: (0, 0)),
            pl.BlockSpec((width, rows), lambda j: (0, 0)),
            pl.BlockSpec((rows, width), lambda j: (0, j)),
        ],
        out_shape=[shaped((rows, width), F32), shaped((width, rows), BF16), shaped((rows, 3 * width), BF16)],
        scratch=[pltpu.VMEM((rows, width), BF16)],
        flops=6 * rows * width * width,
        moved=20 * rows * width,
    )(*blocks, mask, embed, pos, gain, shift, w_qkv, bias)


def own_lanes(value, i, head):
    lane = lax.broadcasted_iota(jnp.int32, value.shape, 1)
    return jnp.where((lane >= i * head) & (lane < (i + 1) * head), value, jnp.zeros_like(value))


def attend_kernel(q_ref, k_ref, v_ref, o_ref, turned_ref, log_ref, *, head):
    factor = head**-0.5 * LOG2_E
    per = LANES // head
    pairs = [slice(at, at + LANES) for at in range(0, q_ref.shape[1], LANES)]
    scores = [[contract(k_ref[:, n], own_lanes(q_ref[:, n], i, head), 1, 1) for i in range(per)] for n in pairs]
    for pair, lanes in enumerate(pairs):
        outs = []
        for i in range(per):
            peak = jnp.max(scores[pair][i], 0, keepdims=True)
            raised = jnp.exp2((scores[pair][i] - peak) * factor)
            total = jnp.sum(raised, 0, keepdims=True)
            mixed = contract(v_ref[:, lanes], raised.astype(BF16), 0, 0)
            outs.append(mixed[i * head : (i + 1) * head] * (1.0 / total))
            log_ref[pair, i : i + 1, :] = peak * factor + jnp.log2(total)
        turned = jnp.concatenate(outs, 0)
        turned_ref[lanes] = turned.astype(BF16)
        o_ref[:, lanes] = turned.T.astype(BF16)


def attend(joint, width):
    rows = joint.shape[0]
    head = width // HEADS
    pairs, per = width // LANES, LANES // head
    some = 2 if pairs % 2 == 0 else 1
    steps = pairs // some
    block = lambda off: pl.BlockSpec((rows, some * LANES), lambda h: (0, h + off))
    return call(
        functools.partial(attend_kernel, head=head),
        grid=(steps,),
        in_specs=[block(0), block(steps), block(2 * steps)],
        out_specs=[
            block(0),
            pl.BlockSpec((some * LANES, rows), lambda h: (h, 0)),
            pl.BlockSpec((some, per, rows), lambda h: (h, 0, 0)),
        ],
        out_shape=[shaped((rows, width), BF16), shaped((width, rows), BF16), shaped((pairs, per, rows), F32)],
        flops=16 * rows * rows * width,
        moved=8 * rows * width,
        exps=rows * rows * HEADS,
    )(joint, joint, joint)


def attend_back_kernel(side_ref, *refs, head, groups):
    per_clip = [refs[4 * c : 4 * c + 4] for c in range(groups)]
    g_ref, out_ref = refs[4 * groups :]
    scale = head**-0.5
    length = per_clip[0][0].shape[0]
    per = LANES // head
    ahead = []
    for c, (q_ref, k_ref, v_ref, log_ref) in enumerate(per_clip):
        rows = slice(c * length, (c + 1) * length)
        for i in range(per):
            q_own, g_own = own_lanes(q_ref[...], i, head), own_lanes(g_ref[rows], i, head)
            ahead.append((q_own, g_own, contract(k_ref[...], q_own, 1, 1), contract(v_ref[...], g_own, 1, 1)))
    for c, (q_ref, k_ref, v_ref, log_ref) in enumerate(per_clip):
        rows = slice(c * length, (c + 1) * length)
        grad_q, grad_k, grad_v = [], 0.0, 0.0
        for i in range(per):
            q_own, g_own, scores, grad_probs = ahead[c * per + i]
            probs = jnp.exp2(scores * (scale * LOG2_E) - log_ref[0, i : i + 1, :])
            delta = jnp.sum(probs * grad_probs, 0, keepdims=True)
            grad_scores = (probs * (grad_probs - delta)).astype(BF16)
            grad_v = grad_v + contract(probs.astype(BF16), g_own, 1, 0)
            grad_q.append(contract(k_ref[...], grad_scores, 0, 0)[i * head : (i + 1) * head])
            grad_k = grad_k + contract(grad_scores, q_own, 1, 0)
        out_ref[0, rows] = (jnp.concatenate(grad_q, 0) * scale).T.astype(BF16)
        out_ref[1, rows] = (grad_k * scale).astype(BF16)
        out_ref[2, rows] = grad_v.astype(BF16)


def attend_back(side, joints, mix, logs):
    rows, width = mix.shape
    groups = len(joints)
    length = rows // groups
    head = width // HEADS
    pairs, per = width // LANES, LANES // head
    half = pairs // 2

    def block(off):
        return pl.BlockSpec((length, LANES), lambda h, s: (0, off + s[0] * half + h))

    clip = [block(0), block(pairs), block(2 * pairs), pl.BlockSpec((1, per, length), lambda h, s: (s[0] * half + h, 0, 0))]
    operands = []
    for joint, log_sum in zip(joints, logs):
        operands += [joint, joint, joint, log_sum]
    return call(
        functools.partial(attend_back_kernel, head=head, groups=groups),
        prefetch=1,
        share=4096,
        grid=(half,),
        in_specs=clip * groups + [pl.BlockSpec((rows, LANES), lambda h, s: (0, s[0] * half + h))],
        out_specs=pl.BlockSpec((3, rows, LANES), lambda h, s: (0, 0, h)),
        out_shape=shaped((3, rows, width // 2), BF16),
        flops=20 * rows * length * width,
        moved=8 * rows * width,
        exps=rows * length * HEADS // 2,
    )(side, *operands, mix)


def gelu_parts(u):
    phi = 0.5 * (1.0 + lax.erf(u * ROOT_HALF))
    return u * phi, phi + u * jnp.exp(-0.5 * u * u) * (1.0 / ROOT_TWO_PI)


def by_segment(refs, values, clip=None):
    clips, seg, _ = refs[0].shape
    for c in range(clips) if clip is None else (clip,):
        for d, ref in enumerate(refs):
            at = ((0 if clip is not None else c) * len(refs) + d) * seg
            ref[c] = values[at : at + seg]


def forward_kernel(*refs, groups, chunk):
    filled, attended = refs[:groups], refs[groups : 2 * groups]
    (w_out_ref, out_bias_ref, gain_ref, shift_ref, down_bias_ref, w_up_ref, up_bias_ref, w_down_ref,
     hidden_ref, turned_ref, act_ref, slope_ref, *block_refs, out_s, normed_s) = refs[2 * groups :]
    rows_all = out_s.shape[0]
    step, last = pl.program_id(0), pl.num_programs(0) - 1

    @pl.when(step == 0)
    def _():
        gain, shift = gain_ref[...].astype(F32), shift_ref[...].astype(F32)
        out_bias, down_bias = out_bias_ref[...].astype(F32), down_bias_ref[...].astype(F32)
        length = filled[0].shape[0]
        for c in range(groups):
            rows = slice(c * length, (c + 1) * length)
            hidden = filled[c][...] + contract(attended[c][...], w_out_ref[...], 1, 0) + out_bias
            unit, _ = norm_parts(hidden)
            normed = (unit * gain + shift).astype(BF16)
            hidden_ref[rows] = hidden
            normed_s[rows] = normed
            turned_ref[:, rows] = normed.T
            out_s[rows] = hidden + down_bias

    w_up, w_down = w_up_ref[...], w_down_ref[...]
    bias = up_bias_ref[...].astype(F32)
    chunks = [slice(at, at + chunk) for at in range(0, rows_all, chunk)]
    ahead = [contract(normed_s[rows], w_up, 1, 0) for rows in chunks]
    for rows, up in zip(chunks, ahead):
        value, slope = gelu_parts(up + bias)
        act = value.astype(BF16)
        act_ref[:, rows] = act.T
        slope_ref[rows] = slope.astype(BF16)
        out_s[rows] += contract(act, w_down, 1, 0)

    @pl.when(step == last)
    def _():
        by_segment(block_refs, out_s[...].astype(BF16))


def forward(filled, attended, w_out, out_bias, gain, shift, down_bias, w_up, up_bias, w_down, tile, chunk, tm):
    groups, (length, width) = len(filled), filled[0].shape
    rows, ff = groups * length, w_up.shape[1]
    vec = fixed((1, width))
    whole = pl.BlockSpec((rows, width), lambda j: (0, 0), pipeline_mode=pl.Buffered(1))
    column = pl.BlockSpec((rows, tile), lambda j: (0, j))
    return call(
        functools.partial(forward_kernel, groups=groups, chunk=chunk),
        grid=(ff // tile,),
        in_specs=[fixed((length, width))] * (2 * groups)
        + [fixed((width, width)), vec, vec, vec, vec]
        + [
            pl.BlockSpec((width, tile), lambda j: (0, j)),
            pl.BlockSpec((1, tile), lambda j: (0, j)),
            pl.BlockSpec((tile, width), lambda j: (j, 0)),
        ],
        out_specs=[whole, fixed((width, rows)), pl.BlockSpec((tile, rows), lambda j: (j, 0)), column]
        + [fixed((groups, length // tm, width))] * tm,
        out_shape=[shaped((rows, width), F32), shaped((width, rows), BF16)]
        + [shaped((ff, rows), BF16), shaped((rows, ff), BF16)]
        + [shaped((groups, length // tm, width), BF16)] * tm,
        scratch=[pltpu.VMEM((rows, width), F32), pltpu.VMEM((rows, width), BF16)],
        flops=4 * rows * width * ff + 2 * rows * width * width,
        moved=14 * rows * width + 4 * rows * ff + 4 * width * ff,
        exps=rows * ff,
    )(*filled, *attended, w_out, out_bias, gain, shift, down_bias, w_up, up_bias, w_down)


def tile_back(turned_ref, cot_ref, act_ref, slope_ref, w_up_ref, w_down_ref, gup_s, norm_s, down_ref, up_ref, bias_ref, chunk):
    w_up, w_down = w_up_ref[...], w_down_ref[...]
    total = jnp.zeros(bias_ref.shape, F32)
    chunks = [slice(at, at + chunk) for at in range(0, cot_ref.shape[0], chunk)]
    ahead = [contract(cot_ref[rows], w_down, 1, 1) for rows in chunks]
    down_ref[...] = contract(act_ref[...], cot_ref[...], 1, 0).astype(BF16)
    for rows, grad_act in zip(chunks, ahead):
        gup = (grad_act * slope_ref[rows].astype(F32)).astype(BF16)
        gup_s[rows] = gup
        total = total + jnp.sum(gup.astype(F32), 0, keepdims=True)
        norm_s[rows] += contract(gup, w_up, 1, 1)
    bias_ref[...] = total
    up_ref[...] = contract(turned_ref[...], gup_s[...], 1, 0).astype(BF16)


def back_first_kernel(side_ref, turned_ref, cot_ref, act_ref, slope_ref, w_up_ref, w_down_ref, norm_ref, down_ref, up_ref, bias_ref, gup_s, *, chunk):
    @pl.when(pl.program_id(0) == 0)
    def _():
        norm_ref[...] = jnp.zeros_like(norm_ref)

    tile_back(turned_ref, cot_ref, act_ref, slope_ref, w_up_ref, w_down_ref, gup_s, norm_ref, down_ref, up_ref, bias_ref, chunk)


def back_last_kernel(side_ref, *refs, groups, chunk):
    attended = refs[:groups]
    (turned_ref, cot_ref, act_ref, slope_ref, w_up_ref, w_down_ref, w_out_ref, gain_ref, hidden_ref, norm_ref,
     down_ref, up_ref, bias_ref, grad_hidden_ref, mix_ref, grad_out_ref, sums_ref, gup_s, norm_s, branch_s) = refs[groups:]

    @pl.when(pl.program_id(0) == 0)
    def _():
        norm_s[...] = norm_ref[...]

    tile_back(turned_ref, cot_ref, act_ref, slope_ref, w_up_ref, w_down_ref, gup_s, norm_s, down_ref, up_ref, bias_ref, chunk)

    @pl.when(pl.program_id(0) == pl.num_programs(0) - 1)
    def _():
        gain = gain_ref[...].astype(F32)
        total = [jnp.zeros_like(gain) for _ in range(4)]
        w_out = w_out_ref[...]
        for r in range(norm_s.shape[0] // chunk):
            rows = slice(r * chunk, (r + 1) * chunk)
            unit, inverse = norm_parts(hidden_ref[rows])
            top, grad_norm = cot_ref[rows].astype(F32), norm_s[rows]
            grad_hidden = top + norm_backward(grad_norm, unit, inverse, gain)
            grad_hidden_ref[rows] = grad_hidden
            branch = grad_hidden.astype(BF16)
            branch_s[rows] = branch
            mix_ref[rows] = contract(branch, w_out, 1, 1).astype(BF16)
            parts = (branch.astype(F32), top, grad_norm * unit, grad_norm)
            total = [t + jnp.sum(p, 0, keepdims=True) for t, p in zip(total, parts)]
        sums_ref[...] = jnp.concatenate(total + [jnp.zeros_like(gain)] * 4, 0)
        length = attended[0].shape[1]
        grad_out = 0.0
        for c in range(groups):
            grad_out = grad_out + contract(attended[c][...], branch_s[c * length : (c + 1) * length], 1, 0)
        grad_out_ref[...] = grad_out.astype(BF16)


def back_specs(rows, width, half, tile):
    steps = half // tile
    column = lambda n: pl.BlockSpec((n, tile), lambda j, s: (0, s[0] * steps + j))
    ins = [fixed((width, rows)), fixed((rows, width))]
    ins += [pl.BlockSpec((tile, rows), lambda j, s: (s[0] * steps + j, 0)), column(rows), column(width)]
    ins.append(pl.BlockSpec((tile, width), lambda j, s: (s[0] * steps + j, 0)))
    outs = [
        pl.BlockSpec((tile, width), lambda j, s: (j, 0)),
        pl.BlockSpec((width, tile), lambda j, s: (0, j)),
        pl.BlockSpec((1, tile), lambda j, s: (0, j)),
    ]
    return ins, outs, [shaped((half, width), BF16), shaped((width, half), BF16), shaped((1, half), F32)]


def back_first(side, normed, cot, act, slope, w_up, w_down, tile, chunk):
    rows, width = cot.shape
    half = w_up.shape[1] // 2
    ins, outs, shapes = back_specs(rows, width, half, tile)
    return call(
        functools.partial(back_first_kernel, chunk=chunk),
        prefetch=1,
        grid=(half // tile,),
        in_specs=ins,
        out_specs=[fixed((rows, width))] + outs,
        out_shape=[shaped((rows, width), F32)] + shapes,
        scratch=[pltpu.VMEM((rows, tile), BF16)],
        flops=8 * rows * width * half,
        moved=8 * rows * width + 4 * rows * half + 8 * width * half,
    )(side, normed, cot, act, slope, w_up, w_down)


def back_last(side, attended, normed, cot, act, slope, w_up, w_down, w_out, gain, hidden, norm, tile, chunk):
    rows, width = cot.shape
    groups = len(attended)
    half = w_up.shape[1] // 2
    ins, outs, shapes = back_specs(rows, width, half, tile)
    whole = lambda n: fixed((n, width))
    return call(
        functools.partial(back_last_kernel, groups=groups, chunk=chunk),
        prefetch=1,
        grid=(half // tile,),
        in_specs=[fixed((width, rows // groups))] * groups + ins + [whole(width), whole(1), whole(rows), whole(rows)],
        out_specs=outs + [whole(rows), whole(rows), whole(width), whole(8)],
        out_shape=shapes
        + [shaped((rows, width), F32), shaped((rows, width), BF16), shaped((width, width), BF16), shaped((8, width), F32)],
        scratch=[pltpu.VMEM((rows, tile), BF16), pltpu.VMEM((rows, width), F32), pltpu.VMEM((rows, width), BF16)],
        flops=8 * rows * width * half + 4 * rows * width * width,
        moved=20 * rows * width + 4 * rows * half + 8 * width * half,
    )(side, *attended, normed, cot, act, slope, w_up, w_down, w_out, gain, hidden, norm)


def joint_part(normed, grad_ref, grad_w_ref, bias_ref):
    length = normed[0].shape[1]
    grad_w = 0.0
    for c, normed_ref in enumerate(normed):
        grad_w = grad_w + contract(normed_ref[...], grad_ref[0, c * length : (c + 1) * length], 1, 0)
    grad_w_ref[...] = grad_w.astype(BF16)
    bias_ref[0] = jnp.sum(grad_ref[0].astype(F32), 0, keepdims=True)


def joint_first_kernel(side_ref, *refs, groups):
    normed, (grad_ref, weight_ref, grad_w_ref, bias_ref, acc_ref) = refs[:groups], refs[groups:]
    joint_part(normed, grad_ref, grad_w_ref, bias_ref)
    part = contract(grad_ref[0], weight_ref[...], 1, 1)

    @pl.when(pl.program_id(0) == 0)
    def _():
        acc_ref[...] = part

    @pl.when(pl.program_id(0) > 0)
    def _():
        acc_ref[...] += part


def joint_last_kernel(side_ref, *refs, groups, tm):
    normed, (grad_ref, weight_ref, acc_ref, grad_hidden_ref, gain_ref) = refs[:groups], refs[groups : groups + 5]
    refs = refs[groups + 5 :]
    filled, masks = refs[:groups], refs[groups : 2 * groups]
    (other_bias_ref, sums_ref, up_other_ref, up_own_ref, grad_out_ref, grad_w_ref, away_ref, kept_ref, *input_refs,
     acc_s, pos_s, bias_s, rest_ref) = refs[2 * groups :]
    core, me = side_ref[0], side_ref[1]
    length, half = normed[0].shape[1], grad_w_ref.shape[1]
    step = pl.program_id(0)
    joint_part(normed, grad_ref, grad_w_ref, bias_s.at[pl.ds(step, 1)])

    @pl.when(step == 0)
    def _():
        acc_s[...] = acc_ref[...] + contract(grad_ref[0], weight_ref[...], 1, 1)

    @pl.when(step == 1)
    def _():
        acc_s[...] += contract(grad_ref[0], weight_ref[...], 1, 1)

    @pl.when(step == 2)
    def _():
        gain = gain_ref[...].astype(F32)
        weight = weight_ref[...]
        total = [jnp.zeros_like(gain) for _ in range(3)]
        clips = [slice(c * length, (c + 1) * length) for c in range(groups)]
        grad_norms = [acc_s[rows] + contract(grad_ref[0, rows], weight, 1, 1) for rows in clips]
        for c, rows in enumerate(clips):
            grad_norm = grad_norms[c]
            unit, inverse = norm_parts(filled[c][...])
            grad_filled = grad_hidden_ref[rows] + norm_backward(grad_norm, unit, inverse, gain)
            masked = masks[c][...] > 0.5
            by_segment(input_refs, jnp.where(masked, 0.0, grad_filled).astype(BF16), c)
            parts = (grad_norm * unit, grad_norm, jnp.where(masked, grad_filled, 0.0))
            total = [t + jnp.sum(p, 0, keepdims=True) for t, p in zip(total, parts)]
            pos_s[...] = grad_filled if c == 0 else pos_s[...] + grad_filled
        seg = length // tm
        shares, share_rows, _ = rest_ref.shape
        pos_rows, some = length // shares, shares // tm
        for d in range(tm):
            own = pos_s[d * seg : (d + 1) * seg].reshape(some, pos_rows, pos_s.shape[1])
            rest_ref[pl.ds((me ^ d) * some, some), :pos_rows] = own.astype(BF16)

        def both(other, mine):
            return jnp.where(core == 0, jnp.concatenate([mine, other], 1), jnp.concatenate([other, mine], 1))

        width = gain.shape[1]
        up = both(up_other_ref[...], up_own_ref[...])
        sums = sums_ref[...]
        lines = [both(other_bias_ref[i], bias_s[i]) for i in (0, 2)] + [sums[0:1]]
        lines += [up[:, i * width : (i + 1) * width] for i in range(up.shape[1] // width)]
        lines += [sums[1:2], total[0], total[1], sums[2:3], sums[3:4], total[2]]
        lines.append(jnp.zeros((shares * (share_rows - pos_rows) - len(lines), width), F32))
        small = jnp.concatenate(lines, 0).reshape(shares, share_rows - pos_rows, width)
        rest_ref[:, pos_rows:] = small.astype(BF16)
        rest, grad_out = rest_ref[...], grad_out_ref[...]
        away_ref[...] = jnp.where(core == 1, grad_out, rest)
        kept_ref[...] = jnp.where(core == 1, rest, grad_out)


def joint_specs(groups, rows, width):
    half = width // 2
    return [fixed((width, rows // groups))] * groups + [
        pl.BlockSpec((1, rows, half), lambda i, s: (i, 0, 0)),
        pl.BlockSpec((width, half), lambda i, s: (0, 2 * i + s[0])),
    ]


def joint_first(side, normed, grads, w_qkv):
    _, rows, half = grads.shape
    groups, width = len(normed), 2 * half
    return call(
        functools.partial(joint_first_kernel, groups=groups),
        prefetch=1,
        share=4096,
        grid=(3,),
        in_specs=joint_specs(groups, rows, width),
        out_specs=[
            pl.BlockSpec((width, half), lambda i, s: (0, i)),
            pl.BlockSpec((1, 1, half), lambda i, s: (i, 0, 0)),
            fixed((rows, width)),
        ],
        out_shape=[shaped((width, 3 * half), BF16), shaped((3, 1, half), F32), shaped((rows, width), F32)],
        flops=6 * rows * width * width,
        moved=12 * rows * width,
    )(side, *normed, grads, w_qkv)


def joint_last(side, normed, grads, w_qkv, acc, grad_hidden, gain, filled, masks, bias, sums, up_other, up_own, grad_out, tm):
    shares = grad_out.shape[0]
    _, rows, half = grads.shape
    groups, width = len(normed), 2 * half
    length = rows // groups
    return call(
        functools.partial(joint_last_kernel, groups=groups, tm=tm),
        prefetch=1,
        share=4096,
        grid=(3,),
        in_specs=joint_specs(groups, rows, width)
        + [fixed((rows, width))] * 2
        + [fixed((1, width))]
        + [fixed((length, width))] * groups
        + [fixed((length, 1))] * groups
        + [fixed((3, 1, half)), fixed((8, width)), fixed(up_other.shape), fixed(up_own.shape)]
        + [fixed(grad_out.shape)],
        out_specs=[
            pl.BlockSpec((width, half), lambda i, s: (0, i)),
            fixed(grad_out.shape),
            fixed(grad_out.shape),
        ]
        + [fixed((groups, length // tm, width))] * tm,
        out_shape=[
            shaped((width, 3 * half), BF16),
            shaped(grad_out.shape, BF16),
            shaped(grad_out.shape, BF16),
        ]
        + [shaped((groups, length // tm, width), BF16)] * tm,
        scratch=[
            pltpu.VMEM((rows, width), F32),
            pltpu.VMEM((length, width), F32),
            pltpu.VMEM((3, 1, half), F32),
            pltpu.VMEM(grad_out.shape, BF16),
        ],
        flops=6 * rows * width * width,
        moved=24 * rows * width,
    )(side, *normed, grads, w_qkv, acc, grad_hidden, gain, *filled, *masks, bias, sums, up_other, up_own, grad_out)


def spot_bits(order, tm):
    return [bits_of(bit) if axis == "tm" else bits_of(tm) + bits_of(bit) - 1 for axis, bit in order]


def shares_of(here_ref, refs, orders, tm, place):
    away = place ^ here_ref[0]
    low = here_ref[1] == 0
    half = len(refs) // 2
    out = []
    for own_ref, other_ref, order in zip(refs[:half], refs[half:], orders):
        index = sum(((away >> b) & 1) << k for k, b in enumerate(spot_bits(order, tm)))
        own, other = own_ref[index], other_ref[index]
        out.append((jnp.where(low, own, other).astype(F32), jnp.where(low, other, own).astype(F32)))
    return out


def place_one_kernel(here_ref, *refs, orders, tm, some):
    down_ref, up_ref = refs[4:]
    width = down_ref.shape[2]
    for u in range(some):
        downs, ups = shares_of(here_ref, refs[:4], orders, tm, pl.program_id(0) * some + u)
        rows = ups[0].shape[0]
        for core in range(2):
            parts = downs[core].shape[1] // width
            for part in range(parts):
                at = (u * parts + part) * rows
                down_ref[core, at : at + rows] = downs[core][:, part * width : (part + 1) * width]
            columns = ups[core].shape[1]
            up_ref[u * rows : (u + 1) * rows, core * columns : (core + 1) * columns] = ups[core]


def place_two_kernel(here_ref, *refs, orders, tm, some):
    qkv_ref, out_ref, pos_ref, small_ref = refs[4:]
    width = out_ref.shape[1]
    half = width // 2
    pos_rows, small_rows = pos_ref.shape[0] // some, small_ref.shape[0] // some
    for u in range(some):
        qkvs, (out, rest) = shares_of(here_ref, refs[:4], orders, tm, pl.program_id(0) * some + u)
        rows = slice(u * out.shape[0], (u + 1) * out.shape[0])
        for core in range(2):
            for i in range(3):
                at = i * width + core * half
                qkv_ref[rows, at : at + half] = qkvs[core][:, i * half : (i + 1) * half]
        out_ref[rows] = out
        pos_ref[u * pos_rows : (u + 1) * pos_rows] = rest[:pos_rows]
        small_ref[u * small_rows : (u + 1) * small_rows] = rest[pos_rows:]


def place(kernel, here, gathered, orders, tm, shapes):
    some = 4
    steps = gathered[0].shape[0] // some

    def cut(shape):
        block = shape[:-2] + (shape[-2] // steps, shape[-1])
        return pl.BlockSpec(block, lambda j, here: (0,) * (len(shape) - 2) + (j, 0))

    return call(
        functools.partial(kernel, orders=orders, tm=tm, some=some),
        prefetch=1,
        grid=(steps,),
        in_specs=[fixed(v.shape) for v in gathered],
        out_specs=[cut(s) for s in shapes],
        out_shape=[shaped(s, F32) for s in shapes],
        moved=sum(6 * v.size for v in gathered),
    )(here, *gathered)


def in_order(here, gathered, orders, tm):
    out = []
    half = len(gathered) // 2
    for own, other, order in zip(gathered[:half], gathered[half:], orders):
        bits = spot_bits(order, tm)
        away = jnp.arange(own.shape[0], dtype=jnp.int32) ^ here[0]
        index = sum(((away >> b) & 1) << k for k, b in enumerate(bits))
        own, other = (jnp.take(x, index, axis=0).astype(F32) for x in (own, other))
        low = here[1] == 0
        out.append(jnp.stack([jnp.where(low, own, other), jnp.where(low, other, own)]))
    return out


def bits_of(size):
    return size.bit_length() - 1


def axis_bits(axis):
    return [(axis, 1 << b) for b in range(bits_of(lax.axis_size(axis)))]


def own_bit(axis, bit):
    return (lax.axis_index(axis) // bit) % 2


def hop(value, axis, bit):
    size = lax.axis_size(axis)
    return lax.ppermute(value, axis, [(i, i ^ bit) for i in range(size)])


def tie(*values):
    return lax.optimization_barrier(values)


def take_clips(values):
    tm = lax.axis_size("tm")
    me = lax.axis_index("tm")
    out = []
    for d in range(tm):
        block = lax.dynamic_index_in_dim(values, me ^ d, 1, keepdims=False)
        out.append(hop(block, "tm", d) if d else block)
    return out


def send_clips(blocks):
    return [hop(block, "tm", d) if d else block for d, block in enumerate(blocks)]


def all_clips(blocks, shape):
    return jnp.stack(unshuffle(blocks), 1).reshape(shape)


def unshuffle(blocks):
    me = lax.axis_index("tm")
    blocks = list(blocks)
    for b in range(bits_of(len(blocks))):
        odd = ((me >> b) & 1) == 1
        blocks = [jnp.where(odd, blocks[i ^ (1 << b)], blocks[i]) for i in range(len(blocks))]
    return blocks


def add_low(a, b):
    return (a.astype(F32) + b.astype(F32)).astype(BF16)


def split_share(value):
    count = bits_of(lax.axis_size("clips")) + bits_of(lax.axis_size("tm")) - 1
    return value.reshape((2,) * count + (value.shape[0] >> count, value.shape[1]))


def side_by_side(value, parts):
    return jnp.concatenate(jnp.split(value, parts, -2), -1)


class Sum:
    def __init__(self, folds):
        self.folds = folds
        clip_bits, self.time_bits = axis_bits("clips")[1:], axis_bits("tm")
        self.names = clip_bits[::-1] + self.time_bits[::-1]
        self.orders = (clip_bits, clip_bits[1:] + clip_bits[:1])
        self.rounds = len(clip_bits) + len(self.time_bits)

    def half(self, pair, names, name, other):
        at = names.index(name)
        mine = own_bit(*name)
        pick = lambda x: lax.dynamic_index_in_dim(x, 1 - mine if other else mine, at, keepdims=False)
        return add_low(*(pick(x) for x in pair))

    def half_of_all(self, index, state, other):
        sides = len(self.orders[0])
        if index < sides:
            names = [[n for n in self.names if n not in order[:index]] for order in self.orders]
            return [self.half(p, n, order[index], other) for p, n, order in zip(state, names, self.orders)]
        names = self.time_bits[index - sides :]
        parts = [self.half(pair, names[::-1], names[0], other) for pair in state]
        if len(parts) > 1:
            parts = [side_by_side(x, n) if n > 1 else x for x, n in zip(parts, self.folds)]
        return [jnp.concatenate(parts, -1) if len(parts) > 1 else parts[0]]

    def split(self, index, state):
        return [(away,) for away in self.half_of_all(index, state, True)] + state

    def send(self, index, state):
        sides = len(self.orders[0])
        names = [o[index] for o in self.orders] if index < sides else [self.time_bits[index - sides]]
        away, state = state[: len(names)], state[len(names) :]
        got = [hop(x, *name) for (x,), name in zip(away, names)]
        return list(zip(self.half_of_all(index, state, False), got))

    def scatter(self, index, state):
        return self.send(index, self.split(index, state))

    def share(self, state):
        return add_low(*state[0])

    def gather_orders(self):
        return [self.time_bits[::-1] + order[::-1] for order in self.orders]

    def gather(self, index, state, cut):
        if index < len(self.time_bits):
            return [(state[0], hop(state[0], *self.time_bits[::-1][index]))]
        names = [order[::-1][index - len(self.time_bits)] for order in self.orders]
        return [(value, hop(value, *name)) for value, name in zip(state, names)]

    def join(self, index, state, cut):
        out = [jnp.concatenate(pair, 0) for pair in state]
        if index == len(self.time_bits) - 1:
            return [out[0][..., :cut], out[0][..., cut:]]
        return out


def on_device(
    patches, mask_index, mask_count, w_qkv, q_bias, v_bias, w_out, out_bias, w_up, up_bias,
    w_down, down_bias, norm1_scale, norm1_shift, norm2_scale, norm2_shift, mask_embed, pos_embed,
    cotangent,
):
    clip_count, seg, width = patches.shape
    ff = w_up.shape[1]
    tm = lax.axis_size("tm")
    me = lax.axis_index("tm")
    length = seg * tm
    groups = clip_count // tm
    by_group = (groups, tm, seg, width)
    tile, chunk = 512, 512

    arrived, grouped = [], patches.reshape(by_group)
    for g in range(groups):
        arrived.append(take_clips(grouped[g : g + 1]))
        grouped, *arrived[g] = tie(grouped, *arrived[g])
    tied, *arrived[-1] = tie(cotangent, *arrived[-1])
    cot = take_clips(tied.reshape(by_group))
    arrived = [[b[0] for b in blocks] for blocks in arrived]

    row = lambda x: x.reshape(1, -1)
    joint_bias = row(jnp.concatenate([q_bias, jnp.zeros_like(q_bias), v_bias]))
    out_bias, up_bias, down_bias, gain1, shift1, gain2, shift2, embed = map(
        row, (out_bias, up_bias, down_bias, norm1_scale, norm1_shift, norm2_scale, norm2_shift, mask_embed)
    )
    starts = (me ^ jnp.arange(tm, dtype=jnp.int32)) * seg
    places = (starts[:, None] + jnp.arange(seg, dtype=jnp.int32)[None, :]).reshape(length)
    pos = jnp.concatenate([lax.dynamic_slice_in_dim(pos_embed, (me ^ d) * seg, seg, 0) for d in range(tm)], 0)
    slots = jnp.arange(mask_index.shape[1], dtype=jnp.int32)
    masks = []
    for g in range(groups):
        index_row = lax.dynamic_index_in_dim(mask_index, g * tm + me, 0, keepdims=False)
        count = lax.dynamic_index_in_dim(mask_count, g * tm + me, 0, keepdims=False)
        hit = (places[:, None] == index_row[None, :]) & (slots < count)[None, :]
        masks.append(jnp.any(hit, axis=1, keepdims=True).astype(F32))

    filled, normed_one, joints, attended, turned, logs = [], [], [], [], [], []
    for g in range(groups):
        f, n, j = project(arrived[g], masks[g], embed, pos, gain1, shift1, w_qkv, joint_bias)
        a, a_turned, log_sum = attend(j, width)
        if g < groups - 1:
            a, *arrived[g + 1] = tie(a, *arrived[g + 1])
        else:
            a, cot[1] = tie(a, cot[1])
        for kept, value in zip((filled, normed_one, joints, attended, turned, logs), (f, n, j, a, a_turned, log_sum)):
            kept.append(value)

    core = own_bit("clips", 1).astype(jnp.int32)
    kept_side = jnp.stack([core, me.astype(jnp.int32)])
    away_side = jnp.stack([1 - core, me.astype(jnp.int32)])
    shares = lax.axis_size("clips") // 2 * tm
    here = jnp.stack([(lax.axis_index("clips") // 2 * tm + me).astype(jnp.int32), core])
    hidden, normed_two, act, slope, *block_out = forward(
        filled, attended, w_out, out_bias, gain2, shift2, down_bias, w_up, up_bias, w_down, 1024, 256, tm
    )
    block_out[0], *cot = tie(block_out[0], *cot)
    cot = jnp.concatenate(cot, 1).reshape(groups * length, width)
    norm_acc, down, up, up_sums_away = back_first(away_side, normed_two, cot, act, slope, w_up, w_down, tile, chunk)
    down_got, up_got = hop(down, "clips", 1), hop(up, "clips", 1)
    down, up, up_sums, grad_hidden, mix, grad_out, sums_two = back_last(
        kept_side, turned, normed_two, cot, act, slope, w_up, w_down, w_out, gain2, hidden, norm_acc, tile, chunk
    )
    one = Sum((2, 1))

    def after(values, *states):
        flat = [x for state in states for pair in state for x in pair]
        tied = list(tie(*values, *flat))
        values, flat = tied[: len(values)], tied[len(values) :]
        back = [[tuple(flat.pop(0) for _ in pair) for pair in state] for state in states]
        return (values, *back)

    state = [tuple(split_share(x) for x in pair) for pair in ((down, down_got), (up, up_got))]
    state = one.split(0, state)
    (mix, *block_out), state = after((mix, *block_out), state)
    state = one.send(0, state)
    block_out = send_clips(block_out)
    grads = attend_back(away_side, joints, mix, logs)
    qkv, bias_sums, acc = joint_first(away_side, normed_one, grads, w_qkv)
    qkv_got = hop(qkv, "clips", 1)
    sent_out = block_out
    (acc, sent_out[1], sent_out[2]), state = after((acc, sent_out[1], sent_out[2]), state)
    state = one.split(1, state)
    (mix, acc), state = after((mix, acc), state)
    state = one.send(1, state)
    grads = attend_back(kept_side, joints, mix, logs)
    (grads, *rest_out), state = after((grads, *sent_out[3:]), state)
    sent_out[3:] = rest_out
    state = one.split(2, state)
    (grads,), state = after((grads,), state)
    state = one.send(2, state)
    qkv, rest_away, rest_kept, *input_grad = joint_last(
        kept_side, normed_one, grads, w_qkv, acc, grad_hidden, gain1, filled, masks, bias_sums, sums_two,
        up_sums_away, up_sums, grad_out.reshape(shares, width // shares, width), tm
    )
    (qkv, rest_away, rest_kept, *input_grad), state = after((qkv, rest_away, rest_kept, *input_grad), state)
    rest_away, rest_kept = rest_away.reshape(width, width), rest_kept.reshape(width, width)
    rest_got = hop(rest_away, "clips", 1)
    two = Sum((1, 1))
    pairs = [tuple(split_share(x) for x in pair) for pair in ((qkv, qkv_got), (rest_kept, rest_got))]
    cut_one, cut_two = ff // 2, 3 * width // 2
    share_rows = pairs[0][0].shape[-2]

    def scatter_steps(group, first):
        steps = [lambda s, i=i: group.split(i, s) for i in range(first, group.rounds)]
        return [(split, lambda s, i=i: group.send(i, s)) for i, split in zip(range(first, group.rounds), steps)]

    def gather_steps(group, cut):
        def prepare(i):
            if i == 0:
                return lambda s: [(group.share(s)[None],)]
            return lambda s: [(x,) for x in group.join(i - 1, s, cut)]

        return [
            (prepare(i), lambda s, i=i: group.gather(i, [x for (x,) in s], cut)) for i in range(group.rounds)
        ]

    def core_steps(group, cut):
        return [
            (
                lambda s: [(x,) for x in group.join(group.rounds - 1, s, cut)],
                lambda s: [(x, hop(x, "clips", 1)) for (x,) in s],
            )
        ]

    steps_one = scatter_steps(one, 3) + gather_steps(one, cut_one) + [None] + core_steps(one, cut_one)
    steps_two = scatter_steps(two, 0) + gather_steps(two, cut_two) + core_steps(two, cut_two)
    outputs = []
    for index in range(max(len(steps_one), len(steps_two))):
        if index == 2:
            block_out = all_clips(sent_out, patches.shape)
            (block_out,), state, pairs = after((block_out,), state, pairs)
        if index == len(steps_two) - 1:
            tied, pairs = after((*sent[3:], *outputs), pairs)
            sent[3:], outputs = tied[: len(sent) - 3], tied[len(sent) - 3 :]
        active = [steps[index] if index < len(steps) else None for steps in (steps_one, steps_two)]
        states = [step[0](x) if step else x for step, x in zip(active, (state, pairs))]
        live = [x for x, step in zip(states, active) if step]
        if index == 3:
            input_grad, *live = after(input_grad, *live)
            sent = send_clips(input_grad)
        elif index in (6, 7):
            sent[8 - index : 9 - index], *live = after(sent[8 - index : 9 - index], *live)
        elif index:
            _, *live = after((), *live)
        live = iter(live)
        state, pairs = (step[1](next(live)) if step else x for step, x in zip(active, states))
        if index == len(steps_one) - 1:
            one_all = [own for own, _ in state] + [other for _, other in state]
            if share_rows % 8 == 0:
                outputs = place(
                    place_one_kernel, here, one_all, one.gather_orders(), tm, ((2, ff // 2, width), (width, ff))
                )
    two_all = [own for own, _ in pairs] + [other for _, other in pairs]
    input_grad = all_clips(sent, patches.shape)

    orders_one, orders_two = one.gather_orders(), two.gather_orders()
    if share_rows % 8 == 0:
        down_sum, up_sum = outputs
        shapes = ((width, 3 * width), (width, width), (length, width), (width - length, width))
        qkv_sum, out_sum, pos_sum, small = place(place_two_kernel, here, two_all, orders_two, tm, shapes)
        down_sum = down_sum.reshape(ff, width)
    else:
        downs, ups = in_order(here, one_all, orders_one, tm)
        qkvs, rests = in_order(here, two_all, orders_two, tm)
        down_sum = jnp.stack(jnp.split(downs, 2, -1), 2).reshape(ff, width)
        up_sum = jnp.concatenate(list(ups.reshape(2, width, ff // 2)), 1)
        qkv_sum = jnp.stack(list(qkvs.reshape(2, width, 3, width // 2)), 2).reshape(width, 3 * width)
        out_sum, rest = rests[0].reshape(width, width), rests[1]
        pos_sum = rest[:, : length // shares].reshape(length, width)
        small = rest[:, length // shares :].reshape(width - length, width)
    v = []
    at = 0
    for n in (1, 1, 1, ff // width, 1, 1, 1, 1, 1, 1):
        v.append(small[at : at + n].reshape(-1))
        at += n
    return (block_out, input_grad, qkv_sum, v[0], v[1], out_sum, v[2], up_sum, v[3], down_sum, v[4],
            v[5], v[6], v[7], v[8], v[9], pos_sum)


def solution(mesh):
    rows = P("clips", "tm", None)
    in_specs = (rows, P("clips", None), P("clips")) + (P(),) * 15 + (rows,)
    out_specs = (rows, rows) + (P(),) * 15
    return jax.shard_map(on_device, mesh=mesh, in_specs=in_specs, out_specs=out_specs, check_vma=False)
```

profile of v0, /device:TPU:0, one launch (start us, length us, event | category | flops | bytes accessed | tf_op | source)
XLA Modules:
  0.0 377.4 jit_solution(4602229386225586456)
XLA Ops:
  2.5 3.0 collective-permute-start
  5.6 2.6 collective-permute-start.1
  9.6 1.3 iota_compare_fusion
  20.0 2.7 collective-permute-done.1
  23.6 3.4 collective-permute-start.3
  28.0 1.4 collective-permute-start.5
  29.4 6.9 %shard_map.314 = (f32[512,768]{1,0:T(8,128)}, bf16[768,512]{1,0:T(8,128)(2,1)}, bf16[512,2304]{1,0:T(8,128)(2,1)}) custom-call(bf16[128,768]{1,0:T(8,128)(2,1)} %bitcast.160, bf16[128,768]{1,0:T(8,128)(2,1)} %bitcast.168, bf16[128,768]{1,0:T(8,128)(2,1)} %bitcast.169, bf16[128,768]{1,0:T(8,128)(2,1)} %bitcast.170, f32[512,1]{1,0:T(8,128)} %copy.58.refs_4_.refs_9_, ...), custom_call_target="tpu_custom_call" | custom-call | flops 1811939328 | bytes 7864320 | tf_op jit(solution)/shard_map/pallas_call | solution.py:91
  36.3 7.2 %shard_map.315 = (bf16[512,768]{1,0:T(8,128)(2,1)}, bf16[768,512]{1,0:T(8,128)(2,1)}, f32[6,2,512]{2,1,0:T(2,128)}) custom-call(bf16[512,2304]{1,0:T(8,128)(2,1)} %get-tuple-element.190.q_ref.k_ref.v_ref.refs_0_.refs_1_.refs_2_, bf16[512,2304]{1,0:T(8,128)(2,1)} %get-tuple-element.190.q_ref.k_ref.v_ref.refs_0_.refs_1_.refs_2_, ...), custom_call_target="tpu_custom_call" | custom-call | flops 3221225472 | bytes 3145728 | tf_op jit(solution)/shard_map/pallas_call | solution.py:140
  44.4 2.6 collective-permute-start.6
  47.9 1.5 collective-permute-start.8
  49.4 7.0 %shard_map.316 = (f32[512,768]{1,0:T(8,128)}, bf16[768,512]{1,0:T(8,128)(2,1)}, bf16[512,2304]{1,0:T(8,128)(2,1)}) custom-call(bf16[128,768]{1,0:T(8,128)(2,1)} %bitcast.161, bf16[128,768]{1,0:T(8,128)(2,1)} %bitcast.171, bf16[128,768]{1,0:T(8,128)(2,1)} %bitcast.172, bf16[128,768]{1,0:T(8,128)(2,1)} %bitcast.173, f32[512,1]{1,0:T(8,128)} %copy.59.refs_4_.refs_10_, ...), custom_call_target="tpu_custom_call" | custom-call | flops 1811939328 | bytes 7864320 | tf_op jit(solution)/shard_map/pallas_call | solution.py:91
  56.4 7.1 %shard_map.317 = (bf16[512,768]{1,0:T(8,128)(2,1)}, bf16[768,512]{1,0:T(8,128)(2,1)}, f32[6,2,512]{2,1,0:T(2,128)}) custom-call(bf16[512,2304]{1,0:T(8,128)(2,1)} %get-tuple-element.206.q_ref.k_ref.v_ref.refs_4_.refs_5_.refs_6_, bf16[512,2304]{1,0:T(8,128)(2,1)} %get-tuple-element.206.q_ref.k_ref.v_ref.refs_4_.refs_5_.refs_6_, ...), custom_call_target="tpu_custom_call" | custom-call | flops 3221225472 | bytes 3145728 | tf_op jit(solution)/shard_map/pallas_call | solution.py:140
  63.5 22.4 %shard_map.318 = (f32[1024,768]{1,0:T(8,128)}, bf16[768,1024]{1,0:T(8,128)(2,1)}, bf16[3072,1024]{1,0:T(8,128)(2,1)}, bf16[1024,3072]{1,0:T(8,128)(2,1)}, bf16[2...) custom-call(f32[512,768]{1,0:T(8,128)} %get-tuple-element.210.refs_0, ...), custom_call_target="tpu_custom_call" | custom-call | flops 10871635968 | bytes 33030144 | tf_op jit(solution)/shard_map/pallas_call | solution.py:270
  87.2 15.9 %shard_map.319 = (f32[1024,768]{1,0:T(8,128)}, bf16[1536,768]{1,0:T(8,128)(2,1)}, bf16[768,1536]{1,0:T(8,128)(2,1)}, f32[1,1536]{1,0:T(1,128)}) custom-call(s32[2]{0:T(128)} %get-tuple-element.409.side_ref, bf16[768,1024]{1,0:T(8,128)(2,1)} %get-tuple-element.216.turned_ref.refs_2_, bf16[1024,768]{1,0:T(8,128)(2,1)} %bitcast.153, ...), custom_call_target="tpu_custom_call" | custom-call | flops 9663676416 | bytes 22020096 | tf_op jit(solution)/shard_map/pallas_call | solution.py:368
  103.6 25.5 %shard_map.320 = (bf16[1536,768]{1,0:T(8,128)(2,1)}, bf16[768,1536]{1,0:T(8,128)(2,1)}, f32[1,1536]{1,0:T(1,128)}, f32[1024,768]{1,0:T(8,128)}, bf16[1024,768]{1...) custom-call(s32[2]{0:T(128)} %get-tuple-element.408.side_ref, bf16[768,512]{1,0:T(8,128)(2,1)} %get-tuple-element.208.refs_0_, ...), custom_call_target="tpu_custom_call" | custom-call | flops 12079595520 | bytes 31457280 | tf_op jit(solution)/shard_map/pallas_call | solution.py:387
  129.2 2.7 fusion.1
  131.9 2.6 fusion
  134.5 1.5 collective-permute-start.13
  136.0 1.5 collective-permute-start.14
  138.6 1.9 collective-permute-start.12
  140.5 11.6 %shard_map.321.refs_2_ = bf16[3,1024,384]{2,1,0:T(8,128)(2,1)} custom-call(s32[2]{0:T(128)} %get-tuple-element.409.side_ref, bf16[512,2304]{1,0:T(8,128)(2,1)} %get-tuple-element.190.q_ref.k_ref.v_ref.refs_0_.refs_1_.refs_2_, bf16[512,2304]{1,0:T(8,128)(2,1)} %get-tuple-element.190.q_ref.k_ref.v_ref.refs_0_.refs_1_.refs_2_, ...), custom_call_target="tpu_custom_call" | custom-call | flops 1966080 | bytes 1536 | tf_op jit(solution)/shard_map/pallas_call | solution.py:199
  152.1 11.0 %shard_map.322 = (bf16[768,1152]{1,0:T(8,128)(2,1)}, f32[3,1,384]{2,1,0:T(1,128)}, f32[1024,768]{1,0:T(8,128)}) custom-call(s32[2]{0:T(128)} %get-tuple-element.409.side_ref, bf16[768,512]{1,0:T(8,128)(2,1)} %get-tuple-element.237.refs_0_, bf16[768,512]{1,0:T(8,128)(2,1)} %get-tuple-element.238.refs_1_, bf16[3,1024,384]{2,1,0:T(8,128)(2,1)} %shard_map.321.refs_2_, ...), custom_call_target="tpu_custom_call" | custom-call | flops 884736 | bytes 2304 | tf_op jit(solution)/shard_map/pallas_call | solution.py:494
  163.2 1.7 fusion.3
  165.1 1.6 fusion.2
  166.7 2.1 fusion.6
  168.9 2.0 fusion.7
  171.9 1.5 collective-permute-start.15
  173.4 11.6 %shard_map.323.refs_2_ = bf16[3,1024,384]{2,1,0:T(8,128)(2,1)} custom-call(s32[2]{0:T(128)} %get-tuple-element.408.side_ref, bf16[512,2304]{1,0:T(8,128)(2,1)} %get-tuple-element.190.q_ref.k_ref.v_ref.refs_0_.refs_1_.refs_2_, bf16[512,2304]{1,0:T(8,128)(2,1)} %get-tuple-element.190.q_ref.k_ref.v_ref.refs_0_.refs_1_.refs_2_, ...), custom_call_target="tpu_custom_call" | custom-call | flops 1966080 | bytes 1536 | tf_op jit(solution)/shard_map/pallas_call | solution.py:199
  188.7 4.9 %collective-permute-start.18 = (bf16[2,48,3072]{2,1,0:T(8,128)(2,1)}, bf16[2,48,3072]{2,1,0:T(8,128)(2,1)}, u32[]{:S(2)}, u32[]{:S(2)}) collective-permute-start(bf16[2,48,3072]{2,1,0:T(8,128)(2,1)} %pad_maximum_fusion.11), channel_id=1, source_target_pairs={{0,1},{1,0},{2,3},{3,2},{4,5},{5,4},{6,7},{7,6},{8,9},{9,8},{10,11... | collective-permute-start | bytes 1769480 | tf_op jit(solution)/shard_map/ppermute | solution.py:645
  193.6 1.7 constant_dynamic-slice_fusion.6
  195.5 1.3 select_bitcast_fusion.7
  196.9 16.4 %shard_map.324 = (bf16[768,1152]{1,0:T(8,128)(2,1)}, bf16[16,48,768]{2,1,0:T(8,128)(2,1)}, bf16[16,48,768]{2,1,0:T(8,128)(2,1)}, bf16[2,128,768]{2,1,0:T(8,128)(...) custom-call(s32[2]{0:T(128)} %get-tuple-element.408.side_ref, ...), custom_call_target="tpu_custom_call" | custom-call | flops 884736 | bytes 4608 | tf_op jit(solution)/shard_map/pallas_call | solution.py:516
  213.4 1.3 copy-done.6
  215.1 1.6 collective-permute-start.21
  218.3 1.6 collective-permute-start.23
  219.9 12.3 %collective-permute-done.19 = bf16[48,3072]{1,0:T(8,128)(2,1)S(1)} collective-permute-done((bf16[48,3072]{1,0:T(8,128)(2,1)S(1)}, bf16[48,3072]{1,0:T(8,128)(2,1)S(1)}, u32[]{:S(2)}, u32[]{:S(2)}) %collective-permute-start.19) | collective-permute-done | bytes 294944 | tf_op jit(solution)/shard_map/ppermute | solution.py:645
  233.4 2.6 collective-permute-done.21
  236.3 1.6 collective-permute-start.25
  238.1 1.2 copy.68
  239.3 1.5 collective-permute-start.26
  241.0 11.9 %collective-permute-done.24 = bf16[1,48,3072]{2,1,0:T(8,128)(2,1)S(1)} collective-permute-done((bf16[1,48,3072]{2,1,0:T(8,128)(2,1)S(1)}, bf16[1,48,3072]{2,1,0:T(8,128)(2,1)S(1)}, u32[]{:S(2)}, u32[]{:S(2)}) %collective-permute-start.24) | collective-permute-done | bytes 294944 | tf_op jit(solution)/shard_map/ppermute | solution.py:645
  253.2 2.0 collective-permute-start.27
  255.4 9.2 %collective-permute-done.28 = bf16[2,48,1920]{2,1,0:T(8,128)(2,1)S(1)} collective-permute-done((bf16[2,48,1920]{2,1,0:T(8,128)(2,1)S(1)}, bf16[2,48,1920]{2,1,0:T(8,128)(2,1)S(1)}, u32[]{:S(2)}, u32[]{:S(2)}) %collective-permute-start.28) | collective-permute-done | bytes 368672 | tf_op jit(solution)/shard_map/ppermute | solution.py:645
  264.7 11.6 %collective-permute-done.27 = bf16[2,48,3072]{2,1,0:T(8,128)(2,1)S(1)} collective-permute-done((bf16[2,48,3072]{2,1,0:T(8,128)(2,1)S(1)}, bf16[2,48,3072]{2,1,0:T(8,128)(2,1)S(1)}, u32[]{:S(2)}, u32[]{:S(2)}) %collective-permute-start.27) | collective-permute-done | bytes 589856 | tf_op jit(solution)/shard_map/ppermute | solution.py:645
  277.1 1.5 collective-permute-start.32
  279.1 8.0 %collective-permute-done.33 = bf16[48,1920]{1,0:T(8,128)(2,1)S(1)} collective-permute-done((bf16[48,1920]{1,0:T(8,128)(2,1)S(1)}, bf16[48,1920]{1,0:T(8,128)(2,1)S(1)}, u32[]{:S(2)}, u32[]{:S(2)}) %collective-permute-start.33) | collective-permute-done | bytes 184352 | tf_op jit(solution)/shard_map/ppermute | solution.py:645
  287.2 4.3 %collective-permute-done.32 = bf16[4,48,1536]{2,1,0:T(8,128)(2,1)S(1)} collective-permute-done((bf16[4,48,1536]{2,1,0:T(8,128)(2,1)S(1)}, bf16[4,48,1536]{2,1,0:T(8,128)(2,1)S(1)}, u32[]{:S(2)}, u32[]{:S(2)}) %collective-permute-start.32) | collective-permute-done | bytes 589856 | tf_op jit(solution)/shard_map/ppermute | solution.py:645
  293.4 2.1 collective-permute-start.36
  296.1 6.5 %collective-permute-done.36 = bf16[1,48,1920]{2,1,0:T(8,128)(2,1)S(1)} collective-permute-done((bf16[1,48,1920]{2,1,0:T(8,128)(2,1)S(1)}, bf16[1,48,1920]{2,1,0:T(8,128)(2,1)S(1)}, u32[]{:S(2)}, u32[]{:S(2)}) %collective-permute-start.36) | collective-permute-done | bytes 184352 | tf_op jit(solution)/shard_map/ppermute | solution.py:645
  302.7 2.7 collective-permute-start.30
  305.4 13.9 %collective-permute-done.37 = bf16[2,48,1920]{2,1,0:T(8,128)(2,1)S(1)} collective-permute-done((bf16[2,48,1920]{2,1,0:T(8,128)(2,1)S(1)}, bf16[2,48,1920]{2,1,0:T(8,128)(2,1)S(1)}, u32[]{:S(2)}, u32[]{:S(2)}) %collective-permute-start.37) | collective-permute-done | bytes 368672 | tf_op jit(solution)/shard_map/ppermute | solution.py:645
  320.5 1.6 pad_maximum_fusion.refs_0_
  322.7 1.5 collective-permute-start.41
  325.8 7.1 %collective-permute-done.42 = bf16[4,48,768]{2,1,0:T(8,128)(2,1)S(1)} collective-permute-done((bf16[4,48,768]{2,1,0:T(8,128)(2,1)S(1)}, bf16[4,48,768]{2,1,0:T(8,128)(2,1)S(1)}, u32[]{:S(2)}, u32[]{:S(2)}) %collective-permute-start.42) | collective-permute-done | bytes 294944 | tf_op jit(solution)/shard_map/ppermute | solution.py:645
  336.2 1.3 collective-permute-start.43
  338.1 1.9 collective-permute-start.29
  340.6 11.4 %shard_map.325 = (f32[2,1536,768]{2,1,0:T(8,128)}, f32[768,3072]{1,0:T(8,128)}) custom-call(s32[2]{0:T(128)} %pad_add_fusion.2.here_ref, bf16[16,48,1536]{2,1,0:T(8,128)(2,1)} %pad_maximum_fusion.refs_0_, bf16[16,48,1536]{2,1,0:T(8,128)(2,1)} %copy-done, bf16[16,48,1536]{2,1,0:T(8,128)(2,1)} %collective-permute-done.38.refs_2_, ...), custom_call_target="tpu_custom_call" | custom-call | bytes 28311552 | tf_op jit(solution)/shard_map/pallas_call | solution.py:607
  352.0 4.7 %collective-permute-done.43 = bf16[8,48,1152]{2,1,0:T(8,128)(2,1)} collective-permute-done((bf16[8,48,1152]{2,1,0:T(8,128)(2,1)S(1)}, bf16[8,48,1152]{2,1,0:T(8,128)(2,1)}, u32[]{:S(2)}, u32[]{:S(2)}) %collective-permute-start.43) | collective-permute-done | bytes 884768 | tf_op jit(solution)/shard_map/ppermute | solution.py:645
  356.6 1.3 pad_maximum_fusion.8.refs_1_
  358.0 1.8 pad_maximum_fusion.2.refs_0_
  361.8 1.2 copy.79
  363.0 2.3 collective-permute-done.46.refs_3_
  366.3 7.8 %shard_map.326 = (f32[768,2304]{1,0:T(8,128)}, f32[768,768]{1,0:T(8,128)}, f32[512,768]{1,0:T(8,128)}, f32[256,768]{1,0:T(8,128)}) custom-call(s32[2]{0:T(128)} %pad_add_fusion.2.here_ref, bf16[16,48,1152]{2,1,0:T(8,128)(2,1)} %copy-done.1, bf16[16,48,768]{2,1,0:T(8,128)(2,1)} %copy-done.2, bf16[16,48,1152]{2,1,0:T(8,128)(2,1)} %collective-permute-done.45.refs_2_, ...), custom_call_target="tpu_custom_call" | custom-call | bytes 17694720 | tf_op jit(solution)/shard_map/pallas_call | solution.py:607
  374.2 1.7 slice_reduce_fusion
  (221 shorter events, 44.2 us)
Async XLA Ops:
  0.7 7.5 %copy-start.24 = (s32[8]{0:T(128)S(1)}, s32[8]{0:T(128)}, u32[]{:S(2)}) copy-start(s32[8]{0:T(128)} %param.21) | copy-start | bytes 100
  0.7 11.4 %copy-start.25 = (bf16[768]{0:T(1024)(128)(2,1)S(1)}, bf16[768]{0:T(1024)(128)(2,1)}, u32[]{:S(2)}) copy-start(bf16[768]{0:T(1024)(128)(2,1)} %param.31) | copy-start | bytes 4612
  0.7 12.0 %copy-start.32 = (bf16[768]{0:T(1024)(128)(2,1)S(1)}, bf16[768]{0:T(1024)(128)(2,1)}, u32[]{:S(2)}) copy-start(bf16[768]{0:T(1024)(128)(2,1)} %param.24) | copy-start | bytes 4612
  0.7 12.0 %copy-start.33 = (bf16[768]{0:T(1024)(128)(2,1)S(1)}, bf16[768]{0:T(1024)(128)(2,1)}, u32[]{:S(2)}) copy-start(bf16[768]{0:T(1024)(128)(2,1)} %param.23) | copy-start | bytes 4612
  0.7 12.6 %copy-start.26 = (bf16[768]{0:T(1024)(128)(2,1)S(1)}, bf16[768]{0:T(1024)(128)(2,1)}, u32[]{:S(2)}) copy-start(bf16[768]{0:T(1024)(128)(2,1)} %param.35) | copy-start | bytes 4612
  0.7 13.2 %copy-start.27 = (bf16[768]{0:T(1024)(128)(2,1)S(1)}, bf16[768]{0:T(1024)(128)(2,1)}, u32[]{:S(2)}) copy-start(bf16[768]{0:T(1024)(128)(2,1)} %param.32) | copy-start | bytes 4612
  0.8 14.6 %copy-start.28 = (bf16[768]{0:T(1024)(128)(2,1)S(1)}, bf16[768]{0:T(1024)(128)(2,1)}, u32[]{:S(2)}) copy-start(bf16[768]{0:T(1024)(128)(2,1)} %param.33) | copy-start | bytes 4612
  0.8 15.2 %copy-start.23 = (bf16[3072]{0:T(1024)(128)(2,1)S(1)}, bf16[3072]{0:T(1024)(128)(2,1)}, u32[]{:S(2)}) copy-start(bf16[3072]{0:T(1024)(128)(2,1)} %param.28) | copy-start | bytes 18436
  0.8 15.8 %copy-start.29 = (bf16[768]{0:T(1024)(128)(2,1)S(1)}, bf16[768]{0:T(1024)(128)(2,1)}, u32[]{:S(2)}) copy-start(bf16[768]{0:T(1024)(128)(2,1)} %param.26) | copy-start | bytes 4612
  0.8 16.4 %copy-start.30 = (bf16[768]{0:T(1024)(128)(2,1)S(1)}, bf16[768]{0:T(1024)(128)(2,1)}, u32[]{:S(2)}) copy-start(bf16[768]{0:T(1024)(128)(2,1)} %param.34) | copy-start | bytes 4612
  0.8 17.0 %copy-start.31 = (bf16[768]{0:T(1024)(128)(2,1)S(1)}, bf16[768]{0:T(1024)(128)(2,1)}, u32[]{:S(2)}) copy-start(bf16[768]{0:T(1024)(128)(2,1)} %param.30) | copy-start | bytes 4612
  0.8 17.5 %copy-start.10 = (bf16[512,768]{1,0:T(8,128)(2,1)S(1)}, bf16[512,768]{1,0:T(8,128)(2,1)}, u32[]{:S(2)}) copy-start(bf16[512,768]{1,0:T(8,128)(2,1)} %param.36) | copy-start | bytes 2359300
  2.5 17.5 %collective-permute-start = (bf16[1,128,768]{2,1,0:T(8,128)(2,1)S(1)}, bf16[1,128,768]{2,1,0:T(8,128)(2,1)S(1)}, u32[]{:S(2)}, u32[]{:S(2)}) collective-permute-start(bf16[1,128,768]{2,1,0:T(8,128)(2,1)S(1)} %get-tuple-element.398), channel_id=1, source_target_pairs={{0,1},{1,0},{2,3},{3,2},{4,5},{5,4},{6,7},{7,6},{8,9},{9,8},{10,11... | collective-permute-start | bytes 589832 | tf_op jit(solution)/shard_map/ppermute | solution.py:645
  5.6 17.2 %collective-permute-start.1 = (bf16[1,128,768]{2,1,0:T(8,128)(2,1)S(1)}, bf16[1,128,768]{2,1,0:T(8,128)(2,1)S(1)}, u32[]{:S(2)}, u32[]{:S(2)}) collective-permute-start(bf16[1,128,768]{2,1,0:T(8,128)(2,1)S(1)} %get-tuple-element.397), channel_id=1, source_target_pairs={{0,2},{1,3},{2,0},{3,1},{4,6},{5,7},{6,4},{7,5},{8,10},{9,11},{10,... | collective-permute-start | bytes 589832 | tf_op jit(solution)/shard_map/ppermute | solution.py:645
  8.1 14.6 %collective-permute-start.2 = (bf16[1,128,768]{2,1,0:T(8,128)(2,1)S(1)}, bf16[1,128,768]{2,1,0:T(8,128)(2,1)S(1)}, u32[]{:S(2)}, u32[]{:S(2)}) collective-permute-start(bf16[1,128,768]{2,1,0:T(8,128)(2,1)S(1)} %get-tuple-element.396), channel_id=1, source_target_pairs={{0,3},{1,2},{2,1},{3,0},{4,7},{5,6},{6,5},{7,4},{8,11},{9,10},{10,... | collective-permute-start | bytes 589832 | tf_op jit(solution)/shard_map/ppermute | solution.py:645
  18.3 4.4 %copy-start.3 = (bf16[8,128,768]{2,1,0:T(8,128)(2,1)S(1)}, bf16[8,128,768]{2,1,0:T(8,128)(2,1)}, u32[]{:S(2)}) copy-start(bf16[8,128,768]{2,1,0:T(8,128)(2,1)} %param.19) | copy-start | bytes 4718596
  23.6 20.0 %collective-permute-start.3 = (bf16[1,128,768]{2,1,0:T(8,128)(2,1)S(1)}, bf16[1,128,768]{2,1,0:T(8,128)(2,1)S(1)}, u32[]{:S(2)}, u32[]{:S(2)}) collective-permute-start(bf16[1,128,768]{2,1,0:T(8,128)(2,1)S(1)} %get-tuple-element.390), channel_id=1, source_target_pairs={{0,1},{1,0},{2,3},{3,2},{4,5},{5,4},{6,7},{7,6},{8,9},{9,8},{10,11... | collective-permute-start | bytes 589832 | tf_op jit(solution)/shard_map/ppermute | solution.py:645
  26.9 16.7 %collective-permute-start.4 = (bf16[1,128,768]{2,1,0:T(8,128)(2,1)S(1)}, bf16[1,128,768]{2,1,0:T(8,128)(2,1)S(1)}, u32[]{:S(2)}, u32[]{:S(2)}) collective-permute-start(bf16[1,128,768]{2,1,0:T(8,128)(2,1)S(1)} %get-tuple-element.389), channel_id=1, source_target_pairs={{0,2},{1,3},{2,0},{3,1},{4,6},{5,7},{6,4},{7,5},{8,10},{9,11},{10,... | collective-permute-start | bytes 589832 | tf_op jit(solution)/shard_map/ppermute | solution.py:645
  28.0 15.6 %collective-permute-start.5 = (bf16[1,128,768]{2,1,0:T(8,128)(2,1)S(1)}, bf16[1,128,768]{2,1,0:T(8,128)(2,1)S(1)}, u32[]{:S(2)}, u32[]{:S(2)}) collective-permute-start(bf16[1,128,768]{2,1,0:T(8,128)(2,1)S(1)} %get-tuple-element.388), channel_id=1, source_target_pairs={{0,3},{1,2},{2,1},{3,0},{4,7},{5,6},{6,5},{7,4},{8,11},{9,10},{10,... | collective-permute-start | bytes 589832 | tf_op jit(solution)/shard_map/ppermute | solution.py:645
  36.3 7.3 %copy-start.7 = (bf16[8,128,768]{2,1,0:T(8,128)(2,1)S(1)}, bf16[8,128,768]{2,1,0:T(8,128)(2,1)}, u32[]{:S(2)}) copy-start(bf16[8,128,768]{2,1,0:T(8,128)(2,1)} %param.37) | copy-start | bytes 4718596
  44.4 19.1 %collective-permute-start.6 = (bf16[2,128,768]{2,1,0:T(8,128)(2,1)S(1)}, bf16[2,128,768]{2,1,0:T(8,128)(2,1)S(1)}, u32[]{:S(2)}, u32[]{:S(2)}) collective-permute-start(bf16[2,128,768]{2,1,0:T(8,128)(2,1)S(1)} %get-tuple-element.381), channel_id=1, source_target_pairs={{0,1},{1,0},{2,3},{3,2},{4,5},{5,4},{6,7},{7,6},{8,9},{9,8},{10,11... | collective-permute-start | bytes 1179656 | tf_op jit(solution)/shard_map/ppermute | solution.py:645
  47.0 38.9 %collective-permute-start.7 = (bf16[2,128,768]{2,1,0:T(8,128)(2,1)S(1)}, bf16[2,128,768]{2,1,0:T(8,128)(2,1)S(1)}, u32[]{:S(2)}, u32[]{:S(2)}) collective-permute-start(bf16[2,128,768]{2,1,0:T(8,128)(2,1)S(1)} %get-tuple-element.379), channel_id=1, source_target_pairs={{0,2},{1,3},{2,0},{3,1},{4,6},{5,7},{6,4},{7,5},{8,10},{9,11},{10,... | collective-permute-start | bytes 1179656 | tf_op jit(solution)/shard_map/ppermute | solution.py:645
  47.9 38.0 %collective-permute-start.8 = (bf16[2,128,768]{2,1,0:T(8,128)(2,1)S(1)}, bf16[2,128,768]{2,1,0:T(8,128)(2,1)S(1)}, u32[]{:S(2)}, u32[]{:S(2)}) collective-permute-start(bf16[2,128,768]{2,1,0:T(8,128)(2,1)S(1)} %get-tuple-element.378), channel_id=1, source_target_pairs={{0,3},{1,2},{2,1},{3,0},{4,7},{5,6},{6,5},{7,4},{8,11},{9,10},{10,... | collective-permute-start | bytes 1179656 | tf_op jit(solution)/shard_map/ppermute | solution.py:645
  103.1 26.1 %collective-permute-start.10 = (bf16[768,1536]{1,0:T(8,128)(2,1)}, bf16[768,1536]{1,0:T(8,128)(2,1)S(1)}, u32[]{:S(2)}, u32[]{:S(2)}) collective-permute-start(bf16[768,1536]{1,0:T(8,128)(2,1)} %get-tuple-element.235), channel_id=1, source_target_pairs={{0,4},{4,0},{8,12},{12,8},{16,20},{20,16},{24,28},{28,24},{1,5},{5... | collective-permute-start | bytes 7077896 | tf_op jit(solution)/shard_map/ppermute | solution.py:645
  103.1 28.8 %collective-permute-start.9 = (bf16[1536,768]{1,0:T(8,128)(2,1)}, bf16[1536,768]{1,0:T(8,128)(2,1)}, u32[]{:S(2)}, u32[]{:S(2)}) collective-permute-start(bf16[1536,768]{1,0:T(8,128)(2,1)} %get-tuple-element.233), channel_id=1, source_target_pairs={{0,4},{4,0},{8,12},{12,8},{16,20},{20,16},{24,28},{28,24},{1,5},{5... | collective-permute-start | bytes 7077896 | tf_op jit(solution)/shard_map/ppermute | solution.py:645
  134.5 32.2 %collective-permute-start.13 = (bf16[2,2,2,96,768]{4,3,1,2,0:T(8,128)(2,1)}, bf16[2,2,2,96,768]{4,3,1,2,0:T(8,128)(2,1)}, u32[]{:S(2)}, u32[]{:S(2)}) collective-permute-start(bf16[2,2,2,96,768]{4,3,1,2,0:T(8,128)(2,1)} %fusion), channel_id=1, source_target_pairs={{0,8},{4,12},{8,0},{12,4},{16,24},{20,28},{24,16},{28,20},{1,9},{5... | collective-permute-start | bytes 3538952 | tf_op jit(solution)/shard_map/ppermute | solution.py:645
  136.0 30.7 %collective-permute-start.14 = (bf16[2,2,2,48,1536]{4,3,1,2,0:T(8,128)(2,1)}, bf16[2,2,2,48,1536]{4,3,1,2,0:T(8,128)(2,1)}, u32[]{:S(2)}, u32[]{:S(2)}) collective-permute-start(bf16[2,2,2,48,1536]{4,3,1,2,0:T(8,128)(2,1)} %fusion.1), channel_id=1, source_target_pairs={{0,16},{4,20},{8,24},{12,28},{16,0},{20,4},{24,8},{28,12},{1,17},{... | collective-permute-start | bytes 3538952 | tf_op jit(solution)/shard_map/ppermute | solution.py:645
  137.5 29.1 %collective-permute-start.11 = (bf16[2,128,768]{2,1,0:T(8,128)(2,1)}, bf16[2,128,768]{2,1,0:T(8,128)(2,1)S(1)}, u32[]{:S(2)}, u32[]{:S(2)}) collective-permute-start(bf16[2,128,768]{2,1,0:T(8,128)(2,1)} %get-tuple-element.240), channel_id=1, source_target_pairs={{0,1},{1,0},{2,3},{3,2},{4,5},{5,4},{6,7},{7,6},{8,9},{9,8},{10,11... | collective-permute-start | bytes 1179656 | tf_op jit(solution)/shard_map/ppermute | solution.py:645
  138.6 28.1 %collective-permute-start.12 = (bf16[2,128,768]{2,1,0:T(8,128)(2,1)}, bf16[2,128,768]{2,1,0:T(8,128)(2,1)}, u32[]{:S(2)}, u32[]{:S(2)}) collective-permute-start(bf16[2,128,768]{2,1,0:T(8,128)(2,1)} %get-tuple-element.241), channel_id=1, source_target_pairs={{0,2},{1,3},{2,0},{3,1},{4,6},{5,7},{6,4},{7,5},{8,10},{9,11},{10,... | collective-permute-start | bytes 1179656 | tf_op jit(solution)/shard_map/ppermute | solution.py:645
  163.1 30.6 %collective-permute-start.20 = (bf16[768,1152]{1,0:T(8,128)(2,1)}, bf16[768,1152]{1,0:T(8,128)(2,1)}, u32[]{:S(2)}, u32[]{:S(2)}) collective-permute-start(bf16[768,1152]{1,0:T(8,128)(2,1)} %get-tuple-element.293), channel_id=1, source_target_pairs={{0,4},{4,0},{8,12},{12,8},{16,20},{20,16},{24,28},{28,24},{1,5},{5... | collective-permute-start | bytes 5308424 | tf_op jit(solution)/shard_map/ppermute | solution.py:645
  170.9 16.6 %collective-permute-start.16 = (bf16[2,2,96,768]{3,2,0,1:T(8,128)(2,1)}, bf16[2,2,96,768]{3,2,0,1:T(8,128)(2,1)S(1)}, u32[]{:S(2)}, u32[]{:S(2)}) collective-permute-start(bf16[2,2,96,768]{3,2,0,1:T(8,128)(2,1)} %fusion.6), channel_id=1, source_target_pairs={{0,16},{4,20},{8,24},{12,28},{16,0},{20,4},{24,8},{28,12},{1,17},{... | collective-permute-start | bytes 1769480 | tf_op jit(solution)/shard_map/ppermute | solution.py:645
  171.4 16.1 %collective-permute-start.17 = (bf16[2,2,48,1536]{3,2,0,1:T(8,128)(2,1)}, bf16[2,2,48,1536]{3,2,0,1:T(8,128)(2,1)S(1)}, u32[]{:S(2)}, u32[]{:S(2)}) collective-permute-start(bf16[2,2,48,1536]{3,2,0,1:T(8,128)(2,1)} %fusion.7), channel_id=1, source_target_pairs={{0,8},{4,12},{8,0},{12,4},{16,24},{20,28},{24,16},{28,20},{1,9},{5... | collective-permute-start | bytes 1769480 | tf_op jit(solution)/shard_map/ppermute | solution.py:645
  171.9 15.5 %collective-permute-start.15 = (bf16[2,128,768]{2,1,0:T(8,128)(2,1)}, bf16[2,128,768]{2,1,0:T(8,128)(2,1)}, u32[]{:S(2)}, u32[]{:S(2)}) collective-permute-start(bf16[2,128,768]{2,1,0:T(8,128)(2,1)} %get-tuple-element.254), channel_id=1, source_target_pairs={{0,3},{1,2},{2,1},{3,0},{4,7},{5,6},{6,5},{7,4},{8,11},{9,10},{10,... | collective-permute-start | bytes 1179656 | tf_op jit(solution)/shard_map/ppermute | solution.py:645
  188.7 24.6 %collective-permute-start.18 = (bf16[2,48,3072]{2,1,0:T(8,128)(2,1)}, bf16[2,48,3072]{2,1,0:T(8,128)(2,1)}, u32[]{:S(2)}, u32[]{:S(2)}) collective-permute-start(bf16[2,48,3072]{2,1,0:T(8,128)(2,1)} %pad_maximum_fusion.11), channel_id=1, source_target_pairs={{0,1},{1,0},{2,3},{3,2},{4,5},{5,4},{6,7},{7,6},{8,9},{9,8},{10,11... | collective-permute-start | bytes 1769480 | tf_op jit(solution)/shard_map/ppermute | solution.py:645
  213.3 4.8 %collective-permute-start.22 = (bf16[768,768]{1,0:T(8,128)(2,1)}, bf16[768,768]{1,0:T(8,128)(2,1)S(1)}, u32[]{:S(2)}, u32[]{:S(2)}) collective-permute-start(bf16[768,768]{1,0:T(8,128)(2,1)} %bitcast.167), channel_id=1, source_target_pairs={{0,4},{4,0},{8,12},{12,8},{16,20},{20,16},{24,28},{28,24},{1,5},{5... | collective-permute-start | bytes 3538952 | tf_op jit(solution)/shard_map/ppermute | solution.py:645
  215.1 20.8 %collective-permute-start.21 = (bf16[2,2,2,48,1152]{4,3,1,2,0:T(8,128)(2,1)S(1)}, bf16[2,2,2,48,1152]{4,3,1,2,0:T(8,128)(2,1)S(1)}, u32[]{:S(2)}, u32[]{:S(2)}) collective-permute-start(bf16[2,2,2,48,1152]{4,3,1,2,0:T(8,128)(2,1)S(1)} %fusion.4), channel_id=1, source_target_pairs={{0,8},{4,12},{8,0},{12,4},{16,24},{20,28},{24,16},{28,20},{1,9},{5... | collective-permute-start | bytes 2654216 | tf_op jit(solution)/shard_map/ppermute | solution.py:645
  217.7 14.6 %collective-permute-start.19 = (bf16[48,3072]{1,0:T(8,128)(2,1)S(1)}, bf16[48,3072]{1,0:T(8,128)(2,1)S(1)}, u32[]{:S(2)}, u32[]{:S(2)}) collective-permute-start(bf16[48,3072]{1,0:T(8,128)(2,1)S(1)} %fusion.22), channel_id=1, source_target_pairs={{0,2},{1,3},{2,0},{3,1},{4,6},{5,7},{6,4},{7,5},{8,10},{9,11},{10,... | collective-permute-start | bytes 884744 | tf_op jit(solution)/shard_map/ppermute | solution.py:645
  218.3 17.8 %collective-permute-start.23 = (bf16[2,2,2,48,768]{4,3,1,2,0:T(8,128)(2,1)S(1)}, bf16[2,2,2,48,768]{4,3,1,2,0:T(8,128)(2,1)S(1)}, u32[]{:S(2)}, u32[]{:S(2)}) collective-permute-start(bf16[2,2,2,48,768]{4,3,1,2,0:T(8,128)(2,1)S(1)} %fusion.10), channel_id=1, source_target_pairs={{0,16},{4,20},{8,24},{12,28},{16,0},{20,4},{24,8},{28,12},{1,17},{... | collective-permute-start | bytes 1769480 | tf_op jit(solution)/shard_map/ppermute | solution.py:645
  236.3 16.7 %collective-permute-start.25 = (bf16[2,2,48,1152]{3,2,0,1:T(8,128)(2,1)S(1)}, bf16[2,2,48,1152]{3,2,0,1:T(8,128)(2,1)S(1)}, u32[]{:S(2)}, u32[]{:S(2)}) collective-permute-start(bf16[2,2,48,1152]{3,2,0,1:T(8,128)(2,1)S(1)} %fusion.15), channel_id=1, source_target_pairs={{0,16},{4,20},{8,24},{12,28},{16,0},{20,4},{24,8},{28,12},{1,17},{... | collective-permute-start | bytes 1327112 | tf_op jit(solution)/shard_map/ppermute | solution.py:645
  239.3 13.6 %collective-permute-start.24 = (bf16[1,48,3072]{2,1,0:T(8,128)(2,1)S(1)}, bf16[1,48,3072]{2,1,0:T(8,128)(2,1)S(1)}, u32[]{:S(2)}, u32[]{:S(2)}) collective-permute-start(bf16[1,48,3072]{2,1,0:T(8,128)(2,1)S(1)} %fusion.24), channel_id=1, source_target_pairs={{0,2},{1,3},{2,0},{3,1},{4,6},{5,7},{6,4},{7,5},{8,10},{9,11},{10,... | collective-permute-start | bytes 884744 | tf_op jit(solution)/shard_map/ppermute | solution.py:645
  239.3 13.6 %collective-permute-start.26 = (bf16[2,2,48,768]{3,2,0,1:T(8,128)(2,1)S(1)}, bf16[2,2,48,768]{3,2,0,1:T(8,128)(2,1)S(1)}, u32[]{:S(2)}, u32[]{:S(2)}) collective-permute-start(bf16[2,2,48,768]{3,2,0,1:T(8,128)(2,1)S(1)} %fusion.25), channel_id=1, source_target_pairs={{0,8},{4,12},{8,0},{12,4},{16,24},{20,28},{24,16},{28,20},{1,9},{5... | collective-permute-start | bytes 884744 | tf_op jit(solution)/shard_map/ppermute | solution.py:645
  253.2 11.5 %collective-permute-start.28 = (bf16[2,48,1920]{2,1,0:T(8,128)(2,1)S(1)}, bf16[2,48,1920]{2,1,0:T(8,128)(2,1)S(1)}, u32[]{:S(2)}, u32[]{:S(2)}) collective-permute-start(bf16[2,48,1920]{2,1,0:T(8,128)(2,1)S(1)} %pad_maximum_fusion.16), channel_id=1, source_target_pairs={{0,1},{1,0},{2,3},{3,2},{4,5},{5,4},{6,7},{7,6},{8,9},{9,8},{10,11... | collective-permute-start | bytes 1105928 | tf_op jit(solution)/shard_map/ppermute | solution.py:645
  253.2 23.1 %collective-permute-start.27 = (bf16[2,48,3072]{2,1,0:T(8,128)(2,1)S(1)}, bf16[2,48,3072]{2,1,0:T(8,128)(2,1)S(1)}, u32[]{:S(2)}, u32[]{:S(2)}) collective-permute-start(bf16[2,48,3072]{2,1,0:T(8,128)(2,1)S(1)} %pad_maximum_fusion.13), channel_id=1, source_target_pairs={{0,1},{1,0},{2,3},{3,2},{4,5},{5,4},{6,7},{7,6},{8,9},{9,8},{10,11... | collective-permute-start | bytes 1769480 | tf_op jit(solution)/shard_map/ppermute | solution.py:645
  276.5 10.6 %collective-permute-start.33 = (bf16[48,1920]{1,0:T(8,128)(2,1)S(1)}, bf16[48,1920]{1,0:T(8,128)(2,1)S(1)}, u32[]{:S(2)}, u32[]{:S(2)}) collective-permute-start(bf16[48,1920]{1,0:T(8,128)(2,1)S(1)} %fusion.28), channel_id=1, source_target_pairs={{0,2},{1,3},{2,0},{3,1},{4,6},{5,7},{6,4},{7,5},{8,10},{9,11},{10,... | collective-permute-start | bytes 552968 | tf_op jit(solution)/shard_map/ppermute | solution.py:645
  277.1 14.4 %collective-permute-start.32 = (bf16[4,48,1536]{2,1,0:T(8,128)(2,1)S(1)}, bf16[4,48,1536]{2,1,0:T(8,128)(2,1)S(1)}, u32[]{:S(2)}, u32[]{:S(2)}) collective-permute-start(bf16[4,48,1536]{2,1,0:T(8,128)(2,1)S(1)} %get-tuple-element.323), channel_id=1, source_target_pairs={{0,8},{4,12},{8,0},{12,4},{16,24},{20,28},{24,16},{28,20},{1,9},{5... | collective-permute-start | bytes 1769480 | tf_op jit(solution)/shard_map/ppermute | solution.py:645
  278.6 14.2 %collective-permute-start.31 = (bf16[4,48,1536]{2,1,0:T(8,128)(2,1)S(1)}, bf16[4,48,1536]{2,1,0:T(8,128)(2,1)S(1)}, u32[]{:S(2)}, u32[]{:S(2)}) collective-permute-start(bf16[4,48,1536]{2,1,0:T(8,128)(2,1)S(1)} %get-tuple-element.322), channel_id=1, source_target_pairs={{0,16},{4,20},{8,24},{12,28},{16,0},{20,4},{24,8},{28,12},{1,17},{... | collective-permute-start | bytes 1769480 | tf_op jit(solution)/shard_map/ppermute | solution.py:645
  291.7 11.0 %copy-start.35 = (bf16[2,128,768]{2,1,0:T(8,128)(2,1)S(1)}, bf16[2,128,768]{2,1,0:T(8,128)(2,1)}, u32[]{:S(2)}) copy-start(bf16[2,128,768]{2,1,0:T(8,128)(2,1)} %get-tuple-element.321) | copy-start | bytes 1179652
  292.9 26.5 %collective-permute-start.35 = (bf16[8,48,1536]{2,1,0:T(8,128)(2,1)S(1)}, bf16[8,48,1536]{2,1,0:T(8,128)(2,1)S(1)}, u32[]{:S(2)}, u32[]{:S(2)}) collective-permute-start(bf16[8,48,1536]{2,1,0:T(8,128)(2,1)S(1)} %pad_maximum_fusion.7), channel_id=1, source_target_pairs={{0,16},{4,20},{8,24},{12,28},{16,0},{20,4},{24,8},{28,12},{1,17},{... | collective-permute-start | bytes 3538952 | tf_op jit(solution)/shard_map/ppermute | solution.py:645
  293.4 9.1 %collective-permute-start.36 = (bf16[1,48,1920]{2,1,0:T(8,128)(2,1)S(1)}, bf16[1,48,1920]{2,1,0:T(8,128)(2,1)S(1)}, u32[]{:S(2)}, u32[]{:S(2)}) collective-permute-start(bf16[1,48,1920]{2,1,0:T(8,128)(2,1)S(1)} %fusion.30), channel_id=1, source_target_pairs={{0,2},{1,3},{2,0},{3,1},{4,6},{5,7},{6,4},{7,5},{8,10},{9,11},{10,... | collective-permute-start | bytes 552968 | tf_op jit(solution)/shard_map/ppermute | solution.py:645
  295.5 25.0 %collective-permute-start.34 = (bf16[8,48,1536]{2,1,0:T(8,128)(2,1)S(1)}, bf16[8,48,1536]{2,1,0:T(8,128)(2,1)S(1)}, u32[]{:S(2)}, u32[]{:S(2)}) collective-permute-start(bf16[8,48,1536]{2,1,0:T(8,128)(2,1)S(1)} %pad_maximum_fusion.6), channel_id=1, source_target_pairs={{0,8},{4,12},{8,0},{12,4},{16,24},{20,28},{24,16},{28,20},{1,9},{5... | collective-permute-start | bytes 3538952 | tf_op jit(solution)/shard_map/ppermute | solution.py:645
  302.6 16.7 %collective-permute-start.37 = (bf16[2,48,1920]{2,1,0:T(8,128)(2,1)S(1)}, bf16[2,48,1920]{2,1,0:T(8,128)(2,1)S(1)}, u32[]{:S(2)}, u32[]{:S(2)}) collective-permute-start(bf16[2,48,1920]{2,1,0:T(8,128)(2,1)S(1)} %pad_maximum_fusion.17), channel_id=1, source_target_pairs={{0,1},{1,0},{2,3},{3,2},{4,5},{5,4},{6,7},{7,6},{8,9},{9,8},{10,11... | collective-permute-start | bytes 1105928 | tf_op jit(solution)/shard_map/ppermute | solution.py:645
  302.7 19.4 %collective-permute-start.30 = (bf16[2,128,768]{2,1,0:T(8,128)(2,1)S(1)}, bf16[2,128,768]{2,1,0:T(8,128)(2,1)S(1)}, u32[]{:S(2)}, u32[]{:S(2)}) collective-permute-start(bf16[2,128,768]{2,1,0:T(8,128)(2,1)S(1)} %copy-done.35), channel_id=1, source_target_pairs={{0,2},{1,3},{2,0},{3,1},{4,6},{5,7},{6,4},{7,5},{8,10},{9,11},{10,... | collective-permute-start | bytes 1179656 | tf_op jit(solution)/shard_map/ppermute | solution.py:645
  319.6 5.3 %copy-start.34 = (bf16[2,128,768]{2,1,0:T(8,128)(2,1)S(1)}, bf16[2,128,768]{2,1,0:T(8,128)(2,1)}, u32[]{:S(2)}) copy-start(bf16[2,128,768]{2,1,0:T(8,128)(2,1)} %get-tuple-element.334) | copy-start | bytes 1179652
  322.1 12.8 %copy-start.19 = (bf16[2,128,768]{2,1,0:T(8,128)(2,1)}, bf16[2,128,768]{2,1,0:T(8,128)(2,1)S(1)}, u32[]{:S(2)}) copy-start(bf16[2,128,768]{2,1,0:T(8,128)(2,1)S(1)} %collective-permute-done.30) | copy-start | bytes 1179652
  322.1 18.5 %collective-permute-start.38 = (bf16[16,48,1536]{2,1,0:T(8,128)(2,1)}, bf16[16,48,1536]{2,1,0:T(8,128)(2,1)}, u32[]{:S(2)}, u32[]{:S(2)}) collective-permute-start(bf16[16,48,1536]{2,1,0:T(8,128)(2,1)} %pad_maximum_fusion.refs_0_), channel_id=1, source_target_pairs={{0,4},{4,0},{8,12},{12,8},{16,20},{20,16},{24,28},{28,24},{1,5},{5... | collective-permute-start | bytes 7077896 | tf_op jit(solution)/shard_map/ppermute | solution.py:645
  322.2 18.4 %collective-permute-start.39 = (bf16[16,48,1536]{2,1,0:T(8,128)(2,1)S(1)}, bf16[16,48,1536]{2,1,0:T(8,128)(2,1)}, u32[]{:S(2)}, u32[]{:S(2)}) collective-permute-start(bf16[16,48,1536]{2,1,0:T(8,128)(2,1)S(1)} %pad_maximum_fusion.1.refs_1_), channel_id=1, source_target_pairs={{0,4},{4,0},{8,12},{12,8},{16,20},{20,16},{24,28},{28,24},{1,5},{5... | collective-permute-start | bytes 7077896 | tf_op jit(solution)/shard_map/ppermute | solution.py:645
  322.7 12.2 %collective-permute-start.41 = (bf16[4,48,1152]{2,1,0:T(8,128)(2,1)S(1)}, bf16[4,48,1152]{2,1,0:T(8,128)(2,1)S(1)}, u32[]{:S(2)}, u32[]{:S(2)}) collective-permute-start(bf16[4,48,1152]{2,1,0:T(8,128)(2,1)S(1)} %fusion.13), channel_id=1, source_target_pairs={{0,16},{4,20},{8,24},{12,28},{16,0},{20,4},{24,8},{28,12},{1,17},{... | collective-permute-start | bytes 1327112 | tf_op jit(solution)/shard_map/ppermute | solution.py:645
  324.2 8.7 %collective-permute-start.42 = (bf16[4,48,768]{2,1,0:T(8,128)(2,1)S(1)}, bf16[4,48,768]{2,1,0:T(8,128)(2,1)S(1)}, u32[]{:S(2)}, u32[]{:S(2)}) collective-permute-start(bf16[4,48,768]{2,1,0:T(8,128)(2,1)S(1)} %pad_maximum_fusion.18), channel_id=1, source_target_pairs={{0,8},{4,12},{8,0},{12,4},{16,24},{20,28},{24,16},{28,20},{1,9},{5... | collective-permute-start | bytes 884744 | tf_op jit(solution)/shard_map/ppermute | solution.py:645
  324.9 10.5 %collective-permute-start.40 = (bf16[2,128,768]{2,1,0:T(8,128)(2,1)S(1)}, bf16[2,128,768]{2,1,0:T(8,128)(2,1)S(1)}, u32[]{:S(2)}, u32[]{:S(2)}) collective-permute-start(bf16[2,128,768]{2,1,0:T(8,128)(2,1)S(1)} %copy-done.34), channel_id=1, source_target_pairs={{0,1},{1,0},{2,3},{3,2},{4,5},{5,4},{6,7},{7,6},{8,9},{9,8},{10,11... | collective-permute-start | bytes 1179656 | tf_op jit(solution)/shard_map/ppermute | solution.py:645
  336.2 20.4 %collective-permute-start.43 = (bf16[8,48,1152]{2,1,0:T(8,128)(2,1)S(1)}, bf16[8,48,1152]{2,1,0:T(8,128)(2,1)}, u32[]{:S(2)}, u32[]{:S(2)}) collective-permute-start(bf16[8,48,1152]{2,1,0:T(8,128)(2,1)S(1)} %pad_maximum_fusion.9), channel_id=1, source_target_pairs={{0,8},{4,12},{8,0},{12,4},{16,24},{20,28},{24,16},{28,20},{1,9},{5... | collective-permute-start | bytes 2654216 | tf_op jit(solution)/shard_map/ppermute | solution.py:645
  337.6 14.4 %collective-permute-start.44 = (bf16[8,48,768]{2,1,0:T(8,128)(2,1)}, bf16[8,48,768]{2,1,0:T(8,128)(2,1)}, u32[]{:S(2)}, u32[]{:S(2)}) collective-permute-start(bf16[8,48,768]{2,1,0:T(8,128)(2,1)} %pad_maximum_fusion.14), channel_id=1, source_target_pairs={{0,16},{4,20},{8,24},{12,28},{16,0},{20,4},{24,8},{28,12},{1,17},{... | collective-permute-start | bytes 1769480 | tf_op jit(solution)/shard_map/ppermute | solution.py:645
  338.1 13.9 %collective-permute-start.29 = (bf16[2,128,768]{2,1,0:T(8,128)(2,1)}, bf16[2,128,768]{2,1,0:T(8,128)(2,1)}, u32[]{:S(2)}, u32[]{:S(2)}) collective-permute-start(bf16[2,128,768]{2,1,0:T(8,128)(2,1)} %get-tuple-element.320), channel_id=1, source_target_pairs={{0,3},{1,2},{2,1},{3,0},{4,7},{5,6},{6,5},{7,4},{8,11},{9,10},{10,... | collective-permute-start | bytes 1179656 | tf_op jit(solution)/shard_map/ppermute | solution.py:645
  359.8 5.5 %collective-permute-start.45 = (bf16[16,48,1152]{2,1,0:T(8,128)(2,1)S(1)}, bf16[16,48,1152]{2,1,0:T(8,128)(2,1)}, u32[]{:S(2)}, u32[]{:S(2)}) collective-permute-start(bf16[16,48,1152]{2,1,0:T(8,128)(2,1)S(1)} %pad_maximum_fusion.2.refs_0_), channel_id=1, source_target_pairs={{0,4},{4,0},{8,12},{12,8},{16,20},{20,16},{24,28},{28,24},{1,5},{5... | collective-permute-start | bytes 5308424 | tf_op jit(solution)/shard_map/ppermute | solution.py:645
  359.9 5.4 %collective-permute-start.46 = (bf16[16,48,768]{2,1,0:T(8,128)(2,1)S(1)}, bf16[16,48,768]{2,1,0:T(8,128)(2,1)S(1)}, u32[]{:S(2)}, u32[]{:S(2)}) collective-permute-start(bf16[16,48,768]{2,1,0:T(8,128)(2,1)S(1)} %pad_maximum_fusion.8.refs_1_), channel_id=1, source_target_pairs={{0,4},{4,0},{8,12},{12,8},{16,20},{20,16},{24,28},{28,24},{1,5},{5... | collective-permute-start | bytes 3538952 | tf_op jit(solution)/shard_map/ppermute | solution.py:645
  (26 other events, 46.2 us)
where the time goes:
time: 385 us; the launch traced here: 377 us
  Pallas kernels  162 us (42%)
  waiting for transfers between devices  101 us (26%)
  starting transfers between devices  55.4 us (14%)
  other arithmetic  34.4 us (9%)
  local copies, waits for them, and re-layouts  22.9 us (6%)
    ppermute x47, waiting for transfers between devices, hop(): return lax.ppermute(value, axis, [(i, i ^ bit) for i in range(size)])  101 us
    ppermute x47, starting transfers between devices, hop(): return lax.ppermute(value, axis, [(i, i ^ bit) for i in range(size)])  55.4 us
    pallas_call x1, Pallas kernels, back_last(): call(functools.partial(back_last_kernel, groups=groups, chunk=chunk), pre...  25.5 us
    pallas_call x2, Pallas kernels, attend_back(): call(functools.partial(attend_back_kernel, head=head, groups=groups), pre...  23.2 us
    pallas_call x1, Pallas kernels, forward(): call(functools.partial(forward_kernel, groups=groups, chunk=chunk), grid=...  22.4 us
    pallas_call x2, Pallas kernels, place(): call(functools.partial(kernel, orders=orders, tm=tm, some=some), prefetch...  19.2 us
    convert_element_type x26, other arithmetic, add_low(): return (a.astype(F32) + b.astype(F32)).astype(BF16)  17.9 us
    pallas_call x1, Pallas kernels, joint_last(): call(functools.partial(joint_last_kernel, groups=groups, tm=tm), prefetch...  16.4 us
  transfers between devices with their start and end apart: 47, of which 19 were waited for; matrix products, arithmetic and copies ran while one was open for 11% of the time, Pallas kernels for 37%

commit v1 on v0

--- a/solution.py
+++ b/solution.py
@@ -226,7 +226,7 @@
 def forward_kernel(*refs, groups, chunk):
     filled, attended = refs[:groups], refs[groups : 2 * groups]
     (w_out_ref, out_bias_ref, gain_ref, shift_ref, down_bias_ref, w_up_ref, up_bias_ref, w_down_ref,
-     hidden_ref, turned_ref, act_ref, slope_ref, *block_refs, out_s, normed_s) = refs[2 * groups :]
+     hidden_ref, turned_ref, act_ref, slope_ref, *block_refs, out_s, normed_s, hidden_s) = refs[2 * groups :]
     rows_all = out_s.shape[0]
     step, last = pl.program_id(0), pl.num_programs(0) - 1
 
@@ -240,13 +240,15 @@
             hidden = filled[c][...] + contract(attended[c][...], w_out_ref[...], 1, 0) + out_bias
             unit, _ = norm_parts(hidden)
             normed = (unit * gain + shift).astype(BF16)
-            hidden_ref[rows] = hidden
+            hidden_s[rows] = hidden
             normed_s[rows] = normed
             turned_ref[:, rows] = normed.T
             out_s[rows] = hidden + down_bias
 
     w_up, w_down = w_up_ref[...], w_down_ref[...]
     bias = up_bias_ref[...].astype(F32)
+    some = hidden_ref.shape[1]
+    hidden_ref[...] = hidden_s[:, pl.ds(pl.multiple_of(step * some, some), some)]
     chunks = [slice(at, at + chunk) for at in range(0, rows_all, chunk)]
     ahead = [contract(normed_s[rows], w_up, 1, 0) for rows in chunks]
     for rows, up in zip(chunks, ahead):
@@ -265,7 +267,6 @@
     groups, (length, width) = len(filled), filled[0].shape
     rows, ff = groups * length, w_up.shape[1]
     vec = fixed((1, width))
-    whole = pl.BlockSpec((rows, width), lambda j: (0, 0), pipeline_mode=pl.Buffered(1))
     column = pl.BlockSpec((rows, tile), lambda j: (0, j))
     return call(
         functools.partial(forward_kernel, groups=groups, chunk=chunk),
@@ -277,16 +278,20 @@
             pl.BlockSpec((1, tile), lambda j: (0, j)),
             pl.BlockSpec((tile, width), lambda j: (j, 0)),
         ],
-        out_specs=[whole, fixed((width, rows)), pl.BlockSpec((tile, rows), lambda j: (j, 0)), column]
+        out_specs=[cut_by_step(rows, width, ff // tile), fixed((width, rows)), pl.BlockSpec((tile, rows), lambda j: (j, 0)), column]
         + [fixed((groups, length // tm, width))] * tm,
         out_shape=[shaped((rows, width), F32), shaped((width, rows), BF16)]
         + [shaped((ff, rows), BF16), shaped((rows, ff), BF16)]
         + [shaped((groups, length // tm, width), BF16)] * tm,
-        scratch=[pltpu.VMEM((rows, width), F32), pltpu.VMEM((rows, width), BF16)],
+        scratch=[pltpu.VMEM((rows, width), F32), pltpu.VMEM((rows, width), BF16), pltpu.VMEM((rows, width), F32)],
         flops=4 * rows * width * ff + 2 * rows * width * width,
         moved=14 * rows * width + 4 * rows * ff + 4 * width * ff,
         exps=rows * ff,
     )(*filled, *attended, w_out, out_bias, gain, shift, down_bias, w_up, up_bias, w_down)
+
+
+def cut_by_step(rows, width, steps):
+    return pl.BlockSpec((rows, width // steps), lambda j, *_: (0, j))
 
 
 def tile_back(turned_ref, cot_ref, act_ref, slope_ref, w_up_ref, w_down_ref, gup_s, norm_s, down_ref, up_ref, bias_ref, chunk):
@@ -315,12 +320,15 @@
 def back_last_kernel(side_ref, *refs, groups, chunk):
     attended = refs[:groups]
     (turned_ref, cot_ref, act_ref, slope_ref, w_up_ref, w_down_ref, w_out_ref, gain_ref, hidden_ref, norm_ref,
-     down_ref, up_ref, bias_ref, grad_hidden_ref, mix_ref, grad_out_ref, sums_ref, gup_s, norm_s, branch_s) = refs[groups:]
+     down_ref, up_ref, bias_ref, grad_hidden_ref, mix_ref, grad_out_ref, sums_ref, gup_s, norm_s, branch_s, hidden_s) = refs[groups:]
 
     @pl.when(pl.program_id(0) == 0)
     def _():
-        norm_s[...] = norm_ref[...]
-
+        norm_s[...] = jnp.zeros_like(norm_s)
+
+    columns = pl.ds(pl.multiple_of(pl.program_id(0) * norm_ref.shape[1], norm_ref.shape[1]), norm_ref.shape[1])
+    hidden_s[:, columns] = hidden_ref[...]
+    norm_s[:, columns] += norm_ref[...]
     tile_back(turned_ref, cot_ref, act_ref, slope_ref, w_up_ref, w_down_ref, gup_s, norm_s, down_ref, up_ref, bias_ref, chunk)
 
     @pl.when(pl.program_id(0) == pl.num_programs(0) - 1)
@@ -330,7 +338,7 @@
         w_out = w_out_ref[...]
         for r in range(norm_s.shape[0] // chunk):
             rows = slice(r * chunk, (r + 1) * chunk)
-            unit, inverse = norm_parts(hidden_ref[rows])
+            unit, inverse = norm_parts(hidden_s[rows])
             top, grad_norm = cot_ref[rows].astype(F32), norm_s[rows]
             grad_hidden = top + norm_backward(grad_norm, unit, inverse, gain)
             grad_hidden_ref[rows] = grad_hidden
@@ -388,11 +396,16 @@
         functools.partial(back_last_kernel, groups=groups, chunk=chunk),
         prefetch=1,
         grid=(half // tile,),
-        in_specs=[fixed((width, rows // groups))] * groups + ins + [whole(width), whole(1), whole(rows), whole(rows)],
+        in_specs=[fixed((width, rows // groups))] * groups + ins + [whole(width), whole(1)] + [cut_by_step(rows, width, half // tile)] * 2,
         out_specs=outs + [whole(rows), whole(rows), whole(width), whole(8)],
         out_shape=shapes
         + [shaped((rows, width), F32), shaped((rows, width), BF16), shaped((width, width), BF16), shaped((8, width), F32)],
-        scratch=[pltpu.VMEM((rows, tile), BF16), pltpu.VMEM((rows, width), F32), pltpu.VMEM((rows, width), BF16)],
+        scratch=[
+            pltpu.VMEM((rows, tile), BF16),
+            pltpu.VMEM((rows, width), F32),
+            pltpu.VMEM((rows, width), BF16),
+            pltpu.VMEM((rows, width), F32),
+        ],
         flops=8 * rows * width * half + 4 * rows * width * width,
         moved=20 * rows * width + 4 * rows * half + 8 * width * half,
     )(side, *attended, normed, cot, act, slope, w_up, w_down, w_out, gain, hidden, norm)
@@ -426,7 +439,7 @@
     refs = refs[groups + 5 :]
     filled, masks = refs[:groups], refs[groups : 2 * groups]
     (other_bias_ref, sums_ref, up_other_ref, up_own_ref, grad_out_ref, grad_w_ref, away_ref, kept_ref, *input_refs,
-     acc_s, pos_s, bias_s, rest_ref) = refs[2 * groups :]
+     acc_s, pos_s, bias_s, rest_ref, hidden_s, filled_s) = refs[2 * groups :]
     core, me = side_ref[0], side_ref[1]
     length, half = normed[0].shape[1], grad_w_ref.shape[1]
     step = pl.program_id(0)
@@ -434,7 +447,14 @@
 
     @pl.when(step == 0)
     def _():
-        acc_s[...] = acc_ref[...] + contract(grad_ref[0], weight_ref[...], 1, 1)
+        acc_s[...] = contract(grad_ref[0], weight_ref[...], 1, 1)
+
+    some = acc_ref.shape[1]
+    columns = pl.ds(pl.multiple_of(step * some, some), some)
+    acc_s[:, columns] += acc_ref[...]
+    hidden_s[:, columns] = grad_hidden_ref[...]
+    for c in range(groups):
+        filled_s[c, :, columns] = filled[c][...]
 
     @pl.when(step == 1)
     def _():
@@ -449,8 +469,8 @@
         grad_norms = [acc_s[rows] + contract(grad_ref[0, rows], weight, 1, 1) for rows in clips]
         for c, rows in enumerate(clips):
             grad_norm = grad_norms[c]
-            unit, inverse = norm_parts(filled[c][...])
-            grad_filled = grad_hidden_ref[rows] + norm_backward(grad_norm, unit, inverse, gain)
+            unit, inverse = norm_parts(filled_s[c])
+            grad_filled = hidden_s[rows] + norm_backward(grad_norm, unit, inverse, gain)
             masked = masks[c][...] > 0.5
             by_segment(input_refs, jnp.where(masked, 0.0, grad_filled).astype(BF16), c)
             parts = (grad_norm * unit, grad_norm, jnp.where(masked, grad_filled, 0.0))
@@ -519,9 +539,9 @@
         share=4096,
         grid=(3,),
         in_specs=joint_specs(groups, rows, width)
-        + [fixed((rows, width))] * 2
+        + [cut_by_step(rows, width, 3)] * 2
         + [fixed((1, width))]
-        + [fixed((length, width))] * groups
+        + [cut_by_step(length, width, 3)] * groups
         + [fixed((length, 1))] * groups
         + [fixed((3, 1, half)), fixed((8, width)), fixed(up_other.shape), fixed(up_own.shape)]
         + [fixed(grad_out.shape)],
@@ -542,6 +562,8 @@
             pltpu.VMEM((length, width), F32),
             pltpu.VMEM((3, 1, half), F32),
             pltpu.VMEM(grad_out.shape, BF16),
+            pltpu.VMEM((rows, width), F32),
+            pltpu.VMEM((groups, length, width), F32),
         ],
         flops=6 * rows * width * width,
         moved=24 * rows * width,
@@ -585,7 +607,10 @@
     half = width // 2
     pos_rows, small_rows = pos_ref.shape[0] // some, small_ref.shape[0] // some
     for u in range(some):
-        qkvs, (out, rest) = shares_of(here_ref, refs[:4], orders, tm, pl.program_id(0) * some + u)
+        lefts, rights = shares_of(here_ref, refs[:4], orders, tm, pl.program_id(0) * some + u)
+        shares = [jnp.concatenate(sides, 1) for sides in zip(lefts, rights)]
+        qkvs = [share[:, : 3 * half] for share in shares]
+        out, rest = [share[:, 3 * half :] for share in shares]
         rows = slice(u * out.shape[0], (u + 1) * out.shape[0])
         for core in range(2):
             for i in range(3):
@@ -847,7 +872,7 @@
     rest_got = hop(rest_away, "clips", 1)
     two = Sum((1, 1))
     pairs = [tuple(split_share(x) for x in pair) for pair in ((qkv, qkv_got), (rest_kept, rest_got))]
-    cut_one, cut_two = ff // 2, 3 * width // 2
+    cut_one, cut_two = ff // 2, -(-5 * width // 4 // LANES) * LANES
     share_rows = pairs[0][0].shape[-2]
 
     def scatter_steps(group, first):
@@ -911,7 +936,8 @@
         down_sum = down_sum.reshape(ff, width)
     else:
         downs, ups = in_order(here, one_all, orders_one, tm)
-        qkvs, rests = in_order(here, two_all, orders_two, tm)
+        both = jnp.concatenate(in_order(here, two_all, orders_two, tm), -1)
+        qkvs, rests = both[..., : 3 * width // 2], both[..., 3 * width // 2 :]
         down_sum = jnp.stack(jnp.split(downs, 2, -1), 2).reshape(ff, width)
         up_sum = jnp.concatenate(list(ups.reshape(2, width, ff // 2)), 1)
         qkv_sum = jnp.stack(list(qkvs.reshape(2, width, 3, width // 2)), 2).reshape(width, 3 * width)

time: 385 us -> 381 us (0.990)
  transfers between devices with their start and end apart: 47 -> 47, of which waited for: 19 -> 18; matrix products, arithmetic and copies ran while one was open for 11% -> 11% of each run, Pallas kernels for 37% -> 37%
where the time goes in v1:
time: 381 us; the launch traced here: 373 us
  Pallas kernels  160 us (42%)
  waiting for transfers between devices  98.7 us (26%)
  starting transfers between devices  55.3 us (15%)
  other arithmetic  34.7 us (9%)
  local copies, waits for them, and re-layouts  22.3 us (6%)
    ppermute x47, waiting for transfers between devices, hop(): return lax.ppermute(value, axis, [(i, i ^ bit) for i in range(size)])  98.7 us
    ppermute x47, starting transfers between devices, hop(): return lax.ppermute(value, axis, [(i, i ^ bit) for i in range(size)])  55.3 us
    pallas_call x1, Pallas kernels, back_last(): call(functools.partial(back_last_kernel, groups=groups, chunk=chunk), pre...  24.9 us
    pallas_call x2, Pallas kernels, attend_back(): call(functools.partial(attend_back_kernel, head=head, groups=groups), pre...  23.2 us
    pallas_call x1, Pallas kernels, forward(): call(functools.partial(forward_kernel, groups=groups, chunk=chunk), grid=...  22 us
    pallas_call x2, Pallas kernels, place(): call(functools.partial(kernel, orders=orders, tm=tm, some=some), prefetch...  19.2 us
    convert_element_type x26, other arithmetic, add_low(): return (a.astype(F32) + b.astype(F32)).astype(BF16)  17.9 us
    pallas_call x1, Pallas kernels, joint_last(): call(functools.partial(joint_last_kernel, groups=groups, tm=tm), prefetch...  15.9 us
  transfers between devices with their start and end apart: 47, of which 18 were waited for; matrix products, arithmetic and copies ran while one was open for 11% of the time, Pallas kernels for 37%

profile of v1, /device:TPU:0, one launch (start us, length us, event | category | flops | bytes accessed | tf_op | source)
XLA Modules:
  0.0 373.2 jit_solution(9779388709634525358)
XLA Ops:
  2.5 3.0 collective-permute-start
  5.6 2.6 collective-permute-start.1
  9.6 1.3 iota_compare_fusion
  20.0 2.7 collective-permute-done.1
  23.6 3.4 collective-permute-start.3
  28.0 1.4 collective-permute-start.5
  29.4 6.9 %shard_map.314 = (f32[512,768]{1,0:T(8,128)}, bf16[768,512]{1,0:T(8,128)(2,1)}, bf16[512,2304]{1,0:T(8,128)(2,1)}) custom-call(bf16[128,768]{1,0:T(8,128)(2,1)} %bitcast.160, bf16[128,768]{1,0:T(8,128)(2,1)} %bitcast.168, bf16[128,768]{1,0:T(8,128)(2,1)} %bitcast.169, bf16[128,768]{1,0:T(8,128)(2,1)} %bitcast.170, f32[512,1]{1,0:T(8,128)} %copy.58.refs_4_.refs_9_, ...), custom_call_target="tpu_custom_call" | custom-call | flops 1811939328 | bytes 7864320 | tf_op jit(solution)/shard_map/pallas_call | solution.py:91
  36.4 7.2 %shard_map.315 = (bf16[512,768]{1,0:T(8,128)(2,1)}, bf16[768,512]{1,0:T(8,128)(2,1)}, f32[6,2,512]{2,1,0:T(2,128)}) custom-call(bf16[512,2304]{1,0:T(8,128)(2,1)} %get-tuple-element.190.q_ref.k_ref.v_ref.refs_0_.refs_1_.refs_2_, bf16[512,2304]{1,0:T(8,128)(2,1)} %get-tuple-element.190.q_ref.k_ref.v_ref.refs_0_.refs_1_.refs_2_, ...), custom_call_target="tpu_custom_call" | custom-call | flops 3221225472 | bytes 3145728 | tf_op jit(solution)/shard_map/pallas_call | solution.py:140
  44.4 2.6 collective-permute-start.6
  48.0 1.5 collective-permute-start.8
  49.4 7.0 %shard_map.316 = (f32[512,768]{1,0:T(8,128)}, bf16[768,512]{1,0:T(8,128)(2,1)}, bf16[512,2304]{1,0:T(8,128)(2,1)}) custom-call(bf16[128,768]{1,0:T(8,128)(2,1)} %bitcast.161, bf16[128,768]{1,0:T(8,128)(2,1)} %bitcast.171, bf16[128,768]{1,0:T(8,128)(2,1)} %bitcast.172, bf16[128,768]{1,0:T(8,128)(2,1)} %bitcast.173, f32[512,1]{1,0:T(8,128)} %copy.59.refs_4_.refs_10_, ...), custom_call_target="tpu_custom_call" | custom-call | flops 1811939328 | bytes 7864320 | tf_op jit(solution)/shard_map/pallas_call | solution.py:91
  56.4 7.1 %shard_map.317 = (bf16[512,768]{1,0:T(8,128)(2,1)}, bf16[768,512]{1,0:T(8,128)(2,1)}, f32[6,2,512]{2,1,0:T(2,128)}) custom-call(bf16[512,2304]{1,0:T(8,128)(2,1)} %get-tuple-element.206.q_ref.k_ref.v_ref.refs_4_.refs_5_.refs_6_, bf16[512,2304]{1,0:T(8,128)(2,1)} %get-tuple-element.206.q_ref.k_ref.v_ref.refs_4_.refs_5_.refs_6_, ...), custom_call_target="tpu_custom_call" | custom-call | flops 3221225472 | bytes 3145728 | tf_op jit(solution)/shard_map/pallas_call | solution.py:140
  63.5 22.0 %shard_map.318 = (f32[1024,768]{1,0:T(8,128)}, bf16[768,1024]{1,0:T(8,128)(2,1)}, bf16[3072,1024]{1,0:T(8,128)(2,1)}, bf16[1024,3072]{1,0:T(8,128)(2,1)}, bf16[2...) custom-call(f32[512,768]{1,0:T(8,128)} %get-tuple-element.210.refs_0, ...), custom_call_target="tpu_custom_call" | custom-call | flops 10871635968 | bytes 33030144 | tf_op jit(solution)/shard_map/pallas_call | solution.py:271
  85.6 1.3 pad_maximum_fusion.2
  86.8 15.9 %shard_map.319 = (f32[1024,768]{1,0:T(8,128)}, bf16[1536,768]{1,0:T(8,128)(2,1)}, bf16[768,1536]{1,0:T(8,128)(2,1)}, f32[1,1536]{1,0:T(1,128)}) custom-call(s32[2]{0:T(128)} %get-tuple-element.409.side_ref, bf16[768,1024]{1,0:T(8,128)(2,1)} %get-tuple-element.216.turned_ref.refs_2_, bf16[1024,768]{1,0:T(8,128)(2,1)} %bitcast.153, ...), custom_call_target="tpu_custom_call" | custom-call | flops 9663676416 | bytes 22020096 | tf_op jit(solution)/shard_map/pallas_call | solution.py:376
  103.2 24.9 %shard_map.320 = (bf16[1536,768]{1,0:T(8,128)(2,1)}, bf16[768,1536]{1,0:T(8,128)(2,1)}, f32[1,1536]{1,0:T(1,128)}, f32[1024,768]{1,0:T(8,128)}, bf16[1024,768]{1...) custom-call(s32[2]{0:T(128)} %get-tuple-element.408.side_ref, bf16[768,512]{1,0:T(8,128)(2,1)} %get-tuple-element.208.refs_0_, ...), custom_call_target="tpu_custom_call" | custom-call | flops 12079595520 | bytes 31457280 | tf_op jit(solution)/shard_map/pallas_call | solution.py:395
  128.2 2.7 fusion.1
  130.9 2.6 fusion
  133.6 1.5 collective-permute-start.13
  135.1 1.5 collective-permute-start.14
  137.6 1.9 collective-permute-start.12
  139.5 11.6 %shard_map.321.refs_2_ = bf16[3,1024,384]{2,1,0:T(8,128)(2,1)} custom-call(s32[2]{0:T(128)} %get-tuple-element.409.side_ref, bf16[512,2304]{1,0:T(8,128)(2,1)} %get-tuple-element.190.q_ref.k_ref.v_ref.refs_0_.refs_1_.refs_2_, bf16[512,2304]{1,0:T(8,128)(2,1)} %get-tuple-element.190.q_ref.k_ref.v_ref.refs_0_.refs_1_.refs_2_, ...), custom_call_target="tpu_custom_call" | custom-call | flops 1966080 | bytes 1536 | tf_op jit(solution)/shard_map/pallas_call | solution.py:199
  151.1 11.0 %shard_map.322 = (bf16[768,1152]{1,0:T(8,128)(2,1)}, f32[3,1,384]{2,1,0:T(1,128)}, f32[1024,768]{1,0:T(8,128)}) custom-call(s32[2]{0:T(128)} %get-tuple-element.409.side_ref, bf16[768,512]{1,0:T(8,128)(2,1)} %get-tuple-element.237.refs_0_, bf16[768,512]{1,0:T(8,128)(2,1)} %get-tuple-element.238.refs_1_, bf16[3,1024,384]{2,1,0:T(8,128)(2,1)} %shard_map.321.refs_2_, ...), custom_call_target="tpu_custom_call" | custom-call | flops 884736 | bytes 2304 | tf_op jit(solution)/shard_map/pallas_call | solution.py:514
  162.2 1.7 fusion.3
  164.1 1.6 fusion.2
  165.8 2.1 fusion.6
  167.9 2.0 fusion.7
  171.0 1.5 collective-permute-start.15
  172.4 11.6 %shard_map.323.refs_2_ = bf16[3,1024,384]{2,1,0:T(8,128)(2,1)} custom-call(s32[2]{0:T(128)} %get-tuple-element.408.side_ref, bf16[512,2304]{1,0:T(8,128)(2,1)} %get-tuple-element.190.q_ref.k_ref.v_ref.refs_0_.refs_1_.refs_2_, bf16[512,2304]{1,0:T(8,128)(2,1)} %get-tuple-element.190.q_ref.k_ref.v_ref.refs_0_.refs_1_.refs_2_, ...), custom_call_target="tpu_custom_call" | custom-call | flops 1966080 | bytes 1536 | tf_op jit(solution)/shard_map/pallas_call | solution.py:199
  187.7 5.0 %collective-permute-start.18 = (bf16[2,48,3072]{2,1,0:T(8,128)(2,1)}, bf16[2,48,3072]{2,1,0:T(8,128)(2,1)}, u32[]{:S(2)}, u32[]{:S(2)}) collective-permute-start(bf16[2,48,3072]{2,1,0:T(8,128)(2,1)} %pad_maximum_fusion.12), channel_id=1, source_target_pairs={{0,1},{1,0},{2,3},{3,2},{4,5},{5,4},{6,7},{7,6},{8,9},{9,8},{10,11... | collective-permute-start | bytes 1769480 | tf_op jit(solution)/shard_map/ppermute | solution.py:670
  192.7 1.7 constant_dynamic-slice_fusion.6
  194.5 1.3 select_bitcast_fusion.7
  195.9 15.9 %shard_map.324 = (bf16[768,1152]{1,0:T(8,128)(2,1)}, bf16[16,48,768]{2,1,0:T(8,128)(2,1)}, bf16[16,48,768]{2,1,0:T(8,128)(2,1)}, bf16[2,128,768]{2,1,0:T(8,128)(...) custom-call(s32[2]{0:T(128)} %get-tuple-element.408.side_ref, ...), custom_call_target="tpu_custom_call" | custom-call | flops 884736 | bytes 4608 | tf_op jit(solution)/shard_map/pallas_call | solution.py:536
  212.0 1.3 copy-done.6
  213.7 1.6 collective-permute-start.21
  216.9 1.6 collective-permute-start.23
  218.6 12.3 %collective-permute-done.19 = bf16[48,3072]{1,0:T(8,128)(2,1)S(1)} collective-permute-done((bf16[48,3072]{1,0:T(8,128)(2,1)S(1)}, bf16[48,3072]{1,0:T(8,128)(2,1)S(1)}, u32[]{:S(2)}, u32[]{:S(2)}) %collective-permute-start.19) | collective-permute-done | bytes 294944 | tf_op jit(solution)/shard_map/ppermute | solution.py:670
  232.0 2.6 collective-permute-done.21
  234.9 1.6 collective-permute-start.25
  237.9 1.5 collective-permute-start.26
  239.6 11.9 %collective-permute-done.24 = bf16[1,48,3072]{2,1,0:T(8,128)(2,1)S(1)} collective-permute-done((bf16[1,48,3072]{2,1,0:T(8,128)(2,1)S(1)}, bf16[1,48,3072]{2,1,0:T(8,128)(2,1)S(1)}, u32[]{:S(2)}, u32[]{:S(2)}) %collective-permute-start.24) | collective-permute-done | bytes 294944 | tf_op jit(solution)/shard_map/ppermute | solution.py:670
  251.8 2.0 collective-permute-start.27
  254.0 9.2 %collective-permute-done.28 = bf16[2,48,1920]{2,1,0:T(8,128)(2,1)S(1)} collective-permute-done((bf16[2,48,1920]{2,1,0:T(8,128)(2,1)S(1)}, bf16[2,48,1920]{2,1,0:T(8,128)(2,1)S(1)}, u32[]{:S(2)}, u32[]{:S(2)}) %collective-permute-start.28) | collective-permute-done | bytes 368672 | tf_op jit(solution)/shard_map/ppermute | solution.py:670
  263.3 11.6 %collective-permute-done.27 = bf16[2,48,3072]{2,1,0:T(8,128)(2,1)S(1)} collective-permute-done((bf16[2,48,3072]{2,1,0:T(8,128)(2,1)S(1)}, bf16[2,48,3072]{2,1,0:T(8,128)(2,1)S(1)}, u32[]{:S(2)}, u32[]{:S(2)}) %collective-permute-start.27) | collective-permute-done | bytes 589856 | tf_op jit(solution)/shard_map/ppermute | solution.py:670
  275.7 1.5 collective-permute-start.32
  277.7 8.0 %collective-permute-done.33 = bf16[48,1920]{1,0:T(8,128)(2,1)S(1)} collective-permute-done((bf16[48,1920]{1,0:T(8,128)(2,1)S(1)}, bf16[48,1920]{1,0:T(8,128)(2,1)S(1)}, u32[]{:S(2)}, u32[]{:S(2)}) %collective-permute-start.33) | collective-permute-done | bytes 184352 | tf_op jit(solution)/shard_map/ppermute | solution.py:670
  285.8 4.3 %collective-permute-done.32 = bf16[4,48,1536]{2,1,0:T(8,128)(2,1)S(1)} collective-permute-done((bf16[4,48,1536]{2,1,0:T(8,128)(2,1)S(1)}, bf16[4,48,1536]{2,1,0:T(8,128)(2,1)S(1)}, u32[]{:S(2)}, u32[]{:S(2)}) %collective-permute-start.32) | collective-permute-done | bytes 589856 | tf_op jit(solution)/shard_map/ppermute | solution.py:670
  292.0 2.1 collective-permute-start.36
  294.7 6.5 %collective-permute-done.36 = bf16[1,48,1920]{2,1,0:T(8,128)(2,1)S(1)} collective-permute-done((bf16[1,48,1920]{2,1,0:T(8,128)(2,1)S(1)}, bf16[1,48,1920]{2,1,0:T(8,128)(2,1)S(1)}, u32[]{:S(2)}, u32[]{:S(2)}) %collective-permute-start.36) | collective-permute-done | bytes 184352 | tf_op jit(solution)/shard_map/ppermute | solution.py:670
  301.3 2.6 collective-permute-start.30
  304.0 13.9 %collective-permute-done.37 = bf16[2,48,1920]{2,1,0:T(8,128)(2,1)S(1)} collective-permute-done((bf16[2,48,1920]{2,1,0:T(8,128)(2,1)S(1)}, bf16[2,48,1920]{2,1,0:T(8,128)(2,1)S(1)}, u32[]{:S(2)}, u32[]{:S(2)}) %collective-permute-start.37) | collective-permute-done | bytes 368672 | tf_op jit(solution)/shard_map/ppermute | solution.py:670
  319.1 1.6 pad_maximum_fusion.refs_0_
  321.9 1.5 collective-permute-start.41
  324.4 6.9 %collective-permute-done.42 = bf16[4,48,896]{2,1,0:T(8,128)(2,1)S(1)} collective-permute-done((bf16[4,48,896]{2,1,0:T(8,128)(2,1)S(1)}, bf16[4,48,896]{2,1,0:T(8,128)(2,1)S(1)}, u32[]{:S(2)}, u32[]{:S(2)}) %collective-permute-start.42) | collective-permute-done | bytes 344096 | tf_op jit(solution)/shard_map/ppermute | solution.py:670
  332.8 1.3 collective-permute-done.40
  334.1 1.3 collective-permute-start.43
  335.9 1.9 collective-permute-start.29
  338.4 11.4 %shard_map.325 = (f32[2,1536,768]{2,1,0:T(8,128)}, f32[768,3072]{1,0:T(8,128)}) custom-call(s32[2]{0:T(128)} %pad_add_fusion.2.here_ref, bf16[16,48,1536]{2,1,0:T(8,128)(2,1)} %pad_maximum_fusion.refs_0_, bf16[16,48,1536]{2,1,0:T(8,128)(2,1)} %copy-done, bf16[16,48,1536]{2,1,0:T(8,128)(2,1)} %collective-permute-done.38.refs_2_, ...), custom_call_target="tpu_custom_call" | custom-call | bytes 28311552 | tf_op jit(solution)/shard_map/pallas_call | solution.py:632
  349.7 1.7 collective-permute-done.44
  352.3 1.4 pad_maximum_fusion.6.refs_1_
  353.7 1.8 pad_maximum_fusion.5.refs_0_
  358.8 2.2 collective-permute-done.46.refs_3_
  362.1 7.8 %shard_map.326 = (f32[768,2304]{1,0:T(8,128)}, f32[768,768]{1,0:T(8,128)}, f32[512,768]{1,0:T(8,128)}, f32[256,768]{1,0:T(8,128)}) custom-call(s32[2]{0:T(128)} %pad_add_fusion.2.here_ref, bf16[16,48,1024]{2,1,0:T(8,128)(2,1)} %copy-done.1, bf16[16,48,896]{2,1,0:T(8,128)(2,1)} %copy-done.2, bf16[16,48,1024]{2,1,0:T(8,128)(2,1)} %collective-permute-done.45.refs_2_, ...), custom_call_target="tpu_custom_call" | custom-call | bytes 17694720 | tf_op jit(solution)/shard_map/pallas_call | solution.py:632
  369.9 1.7 slice_reduce_fusion
  (213 shorter events, 44.7 us)
Async XLA Ops:
  0.7 7.5 %copy-start.20 = (s32[8]{0:T(128)S(1)}, s32[8]{0:T(128)}, u32[]{:S(2)}) copy-start(s32[8]{0:T(128)} %param.21) | copy-start | bytes 100
  0.7 11.4 %copy-start.21 = (bf16[768]{0:T(1024)(128)(2,1)S(1)}, bf16[768]{0:T(1024)(128)(2,1)}, u32[]{:S(2)}) copy-start(bf16[768]{0:T(1024)(128)(2,1)} %param.31) | copy-start | bytes 4612
  0.7 12.0 %copy-start.28 = (bf16[768]{0:T(1024)(128)(2,1)S(1)}, bf16[768]{0:T(1024)(128)(2,1)}, u32[]{:S(2)}) copy-start(bf16[768]{0:T(1024)(128)(2,1)} %param.24) | copy-start | bytes 4612
  0.7 12.0 %copy-start.29 = (bf16[768]{0:T(1024)(128)(2,1)S(1)}, bf16[768]{0:T(1024)(128)(2,1)}, u32[]{:S(2)}) copy-start(bf16[768]{0:T(1024)(128)(2,1)} %param.23) | copy-start | bytes 4612
  0.7 12.6 %copy-start.22 = (bf16[768]{0:T(1024)(128)(2,1)S(1)}, bf16[768]{0:T(1024)(128)(2,1)}, u32[]{:S(2)}) copy-start(bf16[768]{0:T(1024)(128)(2,1)} %param.35) | copy-start | bytes 4612
  0.7 13.2 %copy-start.23 = (bf16[768]{0:T(1024)(128)(2,1)S(1)}, bf16[768]{0:T(1024)(128)(2,1)}, u32[]{:S(2)}) copy-start(bf16[768]{0:T(1024)(128)(2,1)} %param.32) | copy-start | bytes 4612
  0.8 14.6 %copy-start.24 = (bf16[768]{0:T(1024)(128)(2,1)S(1)}, bf16[768]{0:T(1024)(128)(2,1)}, u32[]{:S(2)}) copy-start(bf16[768]{0:T(1024)(128)(2,1)} %param.33) | copy-start | bytes 4612
  0.8 15.2 %copy-start.19 = (bf16[3072]{0:T(1024)(128)(2,1)S(1)}, bf16[3072]{0:T(1024)(128)(2,1)}, u32[]{:S(2)}) copy-start(bf16[3072]{0:T(1024)(128)(2,1)} %param.28) | copy-start | bytes 18436
  0.8 15.8 %copy-start.25 = (bf16[768]{0:T(1024)(128)(2,1)S(1)}, bf16[768]{0:T(1024)(128)(2,1)}, u32[]{:S(2)}) copy-start(bf16[768]{0:T(1024)(128)(2,1)} %param.26) | copy-start | bytes 4612
  0.8 16.4 %copy-start.26 = (bf16[768]{0:T(1024)(128)(2,1)S(1)}, bf16[768]{0:T(1024)(128)(2,1)}, u32[]{:S(2)}) copy-start(bf16[768]{0:T(1024)(128)(2,1)} %param.34) | copy-start | bytes 4612
  0.8 16.9 %copy-start.27 = (bf16[768]{0:T(1024)(128)(2,1)S(1)}, bf16[768]{0:T(1024)(128)(2,1)}, u32[]{:S(2)}) copy-start(bf16[768]{0:T(1024)(128)(2,1)} %param.30) | copy-start | bytes 4612
  0.8 17.5 %copy-start.10 = (bf16[512,768]{1,0:T(8,128)(2,1)S(1)}, bf16[512,768]{1,0:T(8,128)(2,1)}, u32[]{:S(2)}) copy-start(bf16[512,768]{1,0:T(8,128)(2,1)} %param.36) | copy-start | bytes 2359300
  2.5 17.5 %collective-permute-start = (bf16[1,128,768]{2,1,0:T(8,128)(2,1)S(1)}, bf16[1,128,768]{2,1,0:T(8,128)(2,1)S(1)}, u32[]{:S(2)}, u32[]{:S(2)}) collective-permute-start(bf16[1,128,768]{2,1,0:T(8,128)(2,1)S(1)} %get-tuple-element.398), channel_id=1, source_target_pairs={{0,1},{1,0},{2,3},{3,2},{4,5},{5,4},{6,7},{7,6},{8,9},{9,8},{10,11... | collective-permute-start | bytes 589832 | tf_op jit(solution)/shard_map/ppermute | solution.py:670
  5.6 17.2 %collective-permute-start.1 = (bf16[1,128,768]{2,1,0:T(8,128)(2,1)S(1)}, bf16[1,128,768]{2,1,0:T(8,128)(2,1)S(1)}, u32[]{:S(2)}, u32[]{:S(2)}) collective-permute-start(bf16[1,128,768]{2,1,0:T(8,128)(2,1)S(1)} %get-tuple-element.397), channel_id=1, source_target_pairs={{0,2},{1,3},{2,0},{3,1},{4,6},{5,7},{6,4},{7,5},{8,10},{9,11},{10,... | collective-permute-start | bytes 589832 | tf_op jit(solution)/shard_map/ppermute | solution.py:670
  8.1 14.6 %collective-permute-start.2 = (bf16[1,128,768]{2,1,0:T(8,128)(2,1)S(1)}, bf16[1,128,768]{2,1,0:T(8,128)(2,1)S(1)}, u32[]{:S(2)}, u32[]{:S(2)}) collective-permute-start(bf16[1,128,768]{2,1,0:T(8,128)(2,1)S(1)} %get-tuple-element.396), channel_id=1, source_target_pairs={{0,3},{1,2},{2,1},{3,0},{4,7},{5,6},{6,5},{7,4},{8,11},{9,10},{10,... | collective-permute-start | bytes 589832 | tf_op jit(solution)/shard_map/ppermute | solution.py:670
  18.3 4.4 %copy-start.3 = (bf16[8,128,768]{2,1,0:T(8,128)(2,1)S(1)}, bf16[8,128,768]{2,1,0:T(8,128)(2,1)}, u32[]{:S(2)}) copy-start(bf16[8,128,768]{2,1,0:T(8,128)(2,1)} %param.19) | copy-start | bytes 4718596
  23.6 20.0 %collective-permute-start.3 = (bf16[1,128,768]{2,1,0:T(8,128)(2,1)S(1)}, bf16[1,128,768]{2,1,0:T(8,128)(2,1)S(1)}, u32[]{:S(2)}, u32[]{:S(2)}) collective-permute-start(bf16[1,128,768]{2,1,0:T(8,128)(2,1)S(1)} %get-tuple-element.390), channel_id=1, source_target_pairs={{0,1},{1,0},{2,3},{3,2},{4,5},{5,4},{6,7},{7,6},{8,9},{9,8},{10,11... | collective-permute-start | bytes 589832 | tf_op jit(solution)/shard_map/ppermute | solution.py:670
  26.9 16.7 %collective-permute-start.4 = (bf16[1,128,768]{2,1,0:T(8,128)(2,1)S(1)}, bf16[1,128,768]{2,1,0:T(8,128)(2,1)S(1)}, u32[]{:S(2)}, u32[]{:S(2)}) collective-permute-start(bf16[1,128,768]{2,1,0:T(8,128)(2,1)S(1)} %get-tuple-element.389), channel_id=1, source_target_pairs={{0,2},{1,3},{2,0},{3,1},{4,6},{5,7},{6,4},{7,5},{8,10},{9,11},{10,... | collective-permute-start | bytes 589832 | tf_op jit(solution)/shard_map/ppermute | solution.py:670
  28.0 15.6 %collective-permute-start.5 = (bf16[1,128,768]{2,1,0:T(8,128)(2,1)S(1)}, bf16[1,128,768]{2,1,0:T(8,128)(2,1)S(1)}, u32[]{:S(2)}, u32[]{:S(2)}) collective-permute-start(bf16[1,128,768]{2,1,0:T(8,128)(2,1)S(1)} %get-tuple-element.388), channel_id=1, source_target_pairs={{0,3},{1,2},{2,1},{3,0},{4,7},{5,6},{6,5},{7,4},{8,11},{9,10},{10,... | collective-permute-start | bytes 589832 | tf_op jit(solution)/shard_map/ppermute | solution.py:670
  36.4 7.3 %copy-start.7 = (bf16[8,128,768]{2,1,0:T(8,128)(2,1)S(1)}, bf16[8,128,768]{2,1,0:T(8,128)(2,1)}, u32[]{:S(2)}) copy-start(bf16[8,128,768]{2,1,0:T(8,128)(2,1)} %param.37) | copy-start | bytes 4718596
  44.4 19.1 %collective-permute-start.6 = (bf16[2,128,768]{2,1,0:T(8,128)(2,1)S(1)}, bf16[2,128,768]{2,1,0:T(8,128)(2,1)S(1)}, u32[]{:S(2)}, u32[]{:S(2)}) collective-permute-start(bf16[2,128,768]{2,1,0:T(8,128)(2,1)S(1)} %get-tuple-element.381), channel_id=1, source_target_pairs={{0,1},{1,0},{2,3},{3,2},{4,5},{5,4},{6,7},{7,6},{8,9},{9,8},{10,11... | collective-permute-start | bytes 1179656 | tf_op jit(solution)/shard_map/ppermute | solution.py:670
  47.0 38.5 %collective-permute-start.7 = (bf16[2,128,768]{2,1,0:T(8,128)(2,1)S(1)}, bf16[2,128,768]{2,1,0:T(8,128)(2,1)S(1)}, u32[]{:S(2)}, u32[]{:S(2)}) collective-permute-start(bf16[2,128,768]{2,1,0:T(8,128)(2,1)S(1)} %get-tuple-element.379), channel_id=1, source_target_pairs={{0,2},{1,3},{2,0},{3,1},{4,6},{5,7},{6,4},{7,5},{8,10},{9,11},{10,... | collective-permute-start | bytes 1179656 | tf_op jit(solution)/shard_map/ppermute | solution.py:670
  48.0 37.6 %collective-permute-start.8 = (bf16[2,128,768]{2,1,0:T(8,128)(2,1)S(1)}, bf16[2,128,768]{2,1,0:T(8,128)(2,1)S(1)}, u32[]{:S(2)}, u32[]{:S(2)}) collective-permute-start(bf16[2,128,768]{2,1,0:T(8,128)(2,1)S(1)} %get-tuple-element.378), channel_id=1, source_target_pairs={{0,3},{1,2},{2,1},{3,0},{4,7},{5,6},{6,5},{7,4},{8,11},{9,10},{10,... | collective-permute-start | bytes 1179656 | tf_op jit(solution)/shard_map/ppermute | solution.py:670
  102.7 25.5 %collective-permute-start.10 = (bf16[768,1536]{1,0:T(8,128)(2,1)}, bf16[768,1536]{1,0:T(8,128)(2,1)S(1)}, u32[]{:S(2)}, u32[]{:S(2)}) collective-permute-start(bf16[768,1536]{1,0:T(8,128)(2,1)} %get-tuple-element.235), channel_id=1, source_target_pairs={{0,4},{4,0},{8,12},{12,8},{16,20},{20,16},{24,28},{28,24},{1,5},{5... | collective-permute-start | bytes 7077896 | tf_op jit(solution)/shard_map/ppermute | solution.py:670
  102.7 28.2 %collective-permute-start.9 = (bf16[1536,768]{1,0:T(8,128)(2,1)}, bf16[1536,768]{1,0:T(8,128)(2,1)}, u32[]{:S(2)}, u32[]{:S(2)}) collective-permute-start(bf16[1536,768]{1,0:T(8,128)(2,1)} %get-tuple-element.233), channel_id=1, source_target_pairs={{0,4},{4,0},{8,12},{12,8},{16,20},{20,16},{24,28},{28,24},{1,5},{5... | collective-permute-start | bytes 7077896 | tf_op jit(solution)/shard_map/ppermute | solution.py:670
  133.6 32.2 %collective-permute-start.13 = (bf16[2,2,2,96,768]{4,3,1,2,0:T(8,128)(2,1)}, bf16[2,2,2,96,768]{4,3,1,2,0:T(8,128)(2,1)}, u32[]{:S(2)}, u32[]{:S(2)}) collective-permute-start(bf16[2,2,2,96,768]{4,3,1,2,0:T(8,128)(2,1)} %fusion), channel_id=1, source_target_pairs={{0,8},{4,12},{8,0},{12,4},{16,24},{20,28},{24,16},{28,20},{1,9},{5... | collective-permute-start | bytes 3538952 | tf_op jit(solution)/shard_map/ppermute | solution.py:670
  135.1 30.7 %collective-permute-start.14 = (bf16[2,2,2,48,1536]{4,3,1,2,0:T(8,128)(2,1)}, bf16[2,2,2,48,1536]{4,3,1,2,0:T(8,128)(2,1)}, u32[]{:S(2)}, u32[]{:S(2)}) collective-permute-start(bf16[2,2,2,48,1536]{4,3,1,2,0:T(8,128)(2,1)} %fusion.1), channel_id=1, source_target_pairs={{0,16},{4,20},{8,24},{12,28},{16,0},{20,4},{24,8},{28,12},{1,17},{... | collective-permute-start | bytes 3538952 | tf_op jit(solution)/shard_map/ppermute | solution.py:670
  136.6 29.1 %collective-permute-start.11 = (bf16[2,128,768]{2,1,0:T(8,128)(2,1)}, bf16[2,128,768]{2,1,0:T(8,128)(2,1)S(1)}, u32[]{:S(2)}, u32[]{:S(2)}) collective-permute-start(bf16[2,128,768]{2,1,0:T(8,128)(2,1)} %get-tuple-element.240), channel_id=1, source_target_pairs={{0,1},{1,0},{2,3},{3,2},{4,5},{5,4},{6,7},{7,6},{8,9},{9,8},{10,11... | collective-permute-start | bytes 1179656 | tf_op jit(solution)/shard_map/ppermute | solution.py:670
  137.6 28.1 %collective-permute-start.12 = (bf16[2,128,768]{2,1,0:T(8,128)(2,1)}, bf16[2,128,768]{2,1,0:T(8,128)(2,1)}, u32[]{:S(2)}, u32[]{:S(2)}) collective-permute-start(bf16[2,128,768]{2,1,0:T(8,128)(2,1)} %get-tuple-element.241), channel_id=1, source_target_pairs={{0,2},{1,3},{2,0},{3,1},{4,6},{5,7},{6,4},{7,5},{8,10},{9,11},{10,... | collective-permute-start | bytes 1179656 | tf_op jit(solution)/shard_map/ppermute | solution.py:670
  162.1 30.5 %collective-permute-start.20 = (bf16[768,1152]{1,0:T(8,128)(2,1)}, bf16[768,1152]{1,0:T(8,128)(2,1)}, u32[]{:S(2)}, u32[]{:S(2)}) collective-permute-start(bf16[768,1152]{1,0:T(8,128)(2,1)} %get-tuple-element.293), channel_id=1, source_target_pairs={{0,4},{4,0},{8,12},{12,8},{16,20},{20,16},{24,28},{28,24},{1,5},{5... | collective-permute-start | bytes 5308424 | tf_op jit(solution)/shard_map/ppermute | solution.py:670
  165.7 4.2 %copy-start.17 = (bf16[2,128,768]{2,1,0:T(8,128)(2,1)}, bf16[2,128,768]{2,1,0:T(8,128)(2,1)S(1)}, u32[]{:S(2)}) copy-start(bf16[2,128,768]{2,1,0:T(8,128)(2,1)S(1)} %collective-permute-done.11) | copy-start | bytes 1179652
  169.9 16.5 %collective-permute-start.16 = (bf16[2,2,96,768]{3,2,0,1:T(8,128)(2,1)}, bf16[2,2,96,768]{3,2,0,1:T(8,128)(2,1)S(1)}, u32[]{:S(2)}, u32[]{:S(2)}) collective-permute-start(bf16[2,2,96,768]{3,2,0,1:T(8,128)(2,1)} %fusion.6), channel_id=1, source_target_pairs={{0,16},{4,20},{8,24},{12,28},{16,0},{20,4},{24,8},{28,12},{1,17},{... | collective-permute-start | bytes 1769480 | tf_op jit(solution)/shard_map/ppermute | solution.py:670
  170.4 16.1 %collective-permute-start.17 = (bf16[2,2,48,1536]{3,2,0,1:T(8,128)(2,1)}, bf16[2,2,48,1536]{3,2,0,1:T(8,128)(2,1)S(1)}, u32[]{:S(2)}, u32[]{:S(2)}) collective-permute-start(bf16[2,2,48,1536]{3,2,0,1:T(8,128)(2,1)} %fusion.7), channel_id=1, source_target_pairs={{0,8},{4,12},{8,0},{12,4},{16,24},{20,28},{24,16},{28,20},{1,9},{5... | collective-permute-start | bytes 1769480 | tf_op jit(solution)/shard_map/ppermute | solution.py:670
  171.0 15.5 %collective-permute-start.15 = (bf16[2,128,768]{2,1,0:T(8,128)(2,1)}, bf16[2,128,768]{2,1,0:T(8,128)(2,1)}, u32[]{:S(2)}, u32[]{:S(2)}) collective-permute-start(bf16[2,128,768]{2,1,0:T(8,128)(2,1)} %get-tuple-element.254), channel_id=1, source_target_pairs={{0,3},{1,2},{2,1},{3,0},{4,7},{5,6},{6,5},{7,4},{8,11},{9,10},{10,... | collective-permute-start | bytes 1179656 | tf_op jit(solution)/shard_map/ppermute | solution.py:670
  187.7 24.2 %collective-permute-start.18 = (bf16[2,48,3072]{2,1,0:T(8,128)(2,1)}, bf16[2,48,3072]{2,1,0:T(8,128)(2,1)}, u32[]{:S(2)}, u32[]{:S(2)}) collective-permute-start(bf16[2,48,3072]{2,1,0:T(8,128)(2,1)} %pad_maximum_fusion.12), channel_id=1, source_target_pairs={{0,1},{1,0},{2,3},{3,2},{4,5},{5,4},{6,7},{7,6},{8,9},{9,8},{10,11... | collective-permute-start | bytes 1769480 | tf_op jit(solution)/shard_map/ppermute | solution.py:670
  211.9 4.8 %collective-permute-start.22 = (bf16[768,768]{1,0:T(8,128)(2,1)}, bf16[768,768]{1,0:T(8,128)(2,1)S(1)}, u32[]{:S(2)}, u32[]{:S(2)}) collective-permute-start(bf16[768,768]{1,0:T(8,128)(2,1)} %bitcast.167), channel_id=1, source_target_pairs={{0,4},{4,0},{8,12},{12,8},{16,20},{20,16},{24,28},{28,24},{1,5},{5... | collective-permute-start | bytes 3538952 | tf_op jit(solution)/shard_map/ppermute | solution.py:670
  213.7 20.8 %collective-permute-start.21 = (bf16[2,2,2,48,1152]{4,3,1,2,0:T(8,128)(2,1)S(1)}, bf16[2,2,2,48,1152]{4,3,1,2,0:T(8,128)(2,1)S(1)}, u32[]{:S(2)}, u32[]{:S(2)}) collective-permute-start(bf16[2,2,2,48,1152]{4,3,1,2,0:T(8,128)(2,1)S(1)} %fusion.4), channel_id=1, source_target_pairs={{0,8},{4,12},{8,0},{12,4},{16,24},{20,28},{24,16},{28,20},{1,9},{5... | collective-permute-start | bytes 2654216 | tf_op jit(solution)/shard_map/ppermute | solution.py:670
  216.3 14.6 %collective-permute-start.19 = (bf16[48,3072]{1,0:T(8,128)(2,1)S(1)}, bf16[48,3072]{1,0:T(8,128)(2,1)S(1)}, u32[]{:S(2)}, u32[]{:S(2)}) collective-permute-start(bf16[48,3072]{1,0:T(8,128)(2,1)S(1)} %fusion.22), channel_id=1, source_target_pairs={{0,2},{1,3},{2,0},{3,1},{4,6},{5,7},{6,4},{7,5},{8,10},{9,11},{10,... | collective-permute-start | bytes 884744 | tf_op jit(solution)/shard_map/ppermute | solution.py:670
  216.9 17.8 %collective-permute-start.23 = (bf16[2,2,2,48,768]{4,3,1,2,0:T(8,128)(2,1)S(1)}, bf16[2,2,2,48,768]{4,3,1,2,0:T(8,128)(2,1)S(1)}, u32[]{:S(2)}, u32[]{:S(2)}) collective-permute-start(bf16[2,2,2,48,768]{4,3,1,2,0:T(8,128)(2,1)S(1)} %fusion.10), channel_id=1, source_target_pairs={{0,16},{4,20},{8,24},{12,28},{16,0},{20,4},{24,8},{28,12},{1,17},{... | collective-permute-start | bytes 1769480 | tf_op jit(solution)/shard_map/ppermute | solution.py:670
  234.9 16.6 %collective-permute-start.25 = (bf16[2,2,48,1152]{3,2,0,1:T(8,128)(2,1)S(1)}, bf16[2,2,48,1152]{3,2,0,1:T(8,128)(2,1)S(1)}, u32[]{:S(2)}, u32[]{:S(2)}) collective-permute-start(bf16[2,2,48,1152]{3,2,0,1:T(8,128)(2,1)S(1)} %fusion.14), channel_id=1, source_target_pairs={{0,16},{4,20},{8,24},{12,28},{16,0},{20,4},{24,8},{28,12},{1,17},{... | collective-permute-start | bytes 1327112 | tf_op jit(solution)/shard_map/ppermute | solution.py:670
  237.9 13.6 %collective-permute-start.24 = (bf16[1,48,3072]{2,1,0:T(8,128)(2,1)S(1)}, bf16[1,48,3072]{2,1,0:T(8,128)(2,1)S(1)}, u32[]{:S(2)}, u32[]{:S(2)}) collective-permute-start(bf16[1,48,3072]{2,1,0:T(8,128)(2,1)S(1)} %fusion.24), channel_id=1, source_target_pairs={{0,2},{1,3},{2,0},{3,1},{4,6},{5,7},{6,4},{7,5},{8,10},{9,11},{10,... | collective-permute-start | bytes 884744 | tf_op jit(solution)/shard_map/ppermute | solution.py:670
  237.9 13.6 %collective-permute-start.26 = (bf16[2,2,48,768]{3,2,0,1:T(8,128)(2,1)S(1)}, bf16[2,2,48,768]{3,2,0,1:T(8,128)(2,1)S(1)}, u32[]{:S(2)}, u32[]{:S(2)}) collective-permute-start(bf16[2,2,48,768]{3,2,0,1:T(8,128)(2,1)S(1)} %fusion.25), channel_id=1, source_target_pairs={{0,8},{4,12},{8,0},{12,4},{16,24},{20,28},{24,16},{28,20},{1,9},{5... | collective-permute-start | bytes 884744 | tf_op jit(solution)/shard_map/ppermute | solution.py:670
  251.8 11.5 %collective-permute-start.28 = (bf16[2,48,1920]{2,1,0:T(8,128)(2,1)S(1)}, bf16[2,48,1920]{2,1,0:T(8,128)(2,1)S(1)}, u32[]{:S(2)}, u32[]{:S(2)}) collective-permute-start(bf16[2,48,1920]{2,1,0:T(8,128)(2,1)S(1)} %pad_maximum_fusion.16), channel_id=1, source_target_pairs={{0,1},{1,0},{2,3},{3,2},{4,5},{5,4},{6,7},{7,6},{8,9},{9,8},{10,11... | collective-permute-start | bytes 1105928 | tf_op jit(solution)/shard_map/ppermute | solution.py:670
  251.8 23.1 %collective-permute-start.27 = (bf16[2,48,3072]{2,1,0:T(8,128)(2,1)S(1)}, bf16[2,48,3072]{2,1,0:T(8,128)(2,1)S(1)}, u32[]{:S(2)}, u32[]{:S(2)}) collective-permute-start(bf16[2,48,3072]{2,1,0:T(8,128)(2,1)S(1)} %pad_maximum_fusion.14), channel_id=1, source_target_pairs={{0,1},{1,0},{2,3},{3,2},{4,5},{5,4},{6,7},{7,6},{8,9},{9,8},{10,11... | collective-permute-start | bytes 1769480 | tf_op jit(solution)/shard_map/ppermute | solution.py:670
  275.1 10.6 %collective-permute-start.33 = (bf16[48,1920]{1,0:T(8,128)(2,1)S(1)}, bf16[48,1920]{1,0:T(8,128)(2,1)S(1)}, u32[]{:S(2)}, u32[]{:S(2)}) collective-permute-start(bf16[48,1920]{1,0:T(8,128)(2,1)S(1)} %fusion.28), channel_id=1, source_target_pairs={{0,2},{1,3},{2,0},{3,1},{4,6},{5,7},{6,4},{7,5},{8,10},{9,11},{10,... | collective-permute-start | bytes 552968 | tf_op jit(solution)/shard_map/ppermute | solution.py:670
  275.7 14.4 %collective-permute-start.32 = (bf16[4,48,1536]{2,1,0:T(8,128)(2,1)S(1)}, bf16[4,48,1536]{2,1,0:T(8,128)(2,1)S(1)}, u32[]{:S(2)}, u32[]{:S(2)}) collective-permute-start(bf16[4,48,1536]{2,1,0:T(8,128)(2,1)S(1)} %get-tuple-element.323), channel_id=1, source_target_pairs={{0,8},{4,12},{8,0},{12,4},{16,24},{20,28},{24,16},{28,20},{1,9},{5... | collective-permute-start | bytes 1769480 | tf_op jit(solution)/shard_map/ppermute | solution.py:670
  277.2 14.2 %collective-permute-start.31 = (bf16[4,48,1536]{2,1,0:T(8,128)(2,1)S(1)}, bf16[4,48,1536]{2,1,0:T(8,128)(2,1)S(1)}, u32[]{:S(2)}, u32[]{:S(2)}) collective-permute-start(bf16[4,48,1536]{2,1,0:T(8,128)(2,1)S(1)} %get-tuple-element.322), channel_id=1, source_target_pairs={{0,16},{4,20},{8,24},{12,28},{16,0},{20,4},{24,8},{28,12},{1,17},{... | collective-permute-start | bytes 1769480 | tf_op jit(solution)/shard_map/ppermute | solution.py:670
  290.3 11.0 %copy-start.31 = (bf16[2,128,768]{2,1,0:T(8,128)(2,1)S(1)}, bf16[2,128,768]{2,1,0:T(8,128)(2,1)}, u32[]{:S(2)}) copy-start(bf16[2,128,768]{2,1,0:T(8,128)(2,1)} %get-tuple-element.321) | copy-start | bytes 1179652
  291.5 26.5 %collective-permute-start.35 = (bf16[8,48,1536]{2,1,0:T(8,128)(2,1)S(1)}, bf16[8,48,1536]{2,1,0:T(8,128)(2,1)S(1)}, u32[]{:S(2)}, u32[]{:S(2)}) collective-permute-start(bf16[8,48,1536]{2,1,0:T(8,128)(2,1)S(1)} %pad_maximum_fusion.8), channel_id=1, source_target_pairs={{0,16},{4,20},{8,24},{12,28},{16,0},{20,4},{24,8},{28,12},{1,17},{... | collective-permute-start | bytes 3538952 | tf_op jit(solution)/shard_map/ppermute | solution.py:670
  292.0 9.1 %collective-permute-start.36 = (bf16[1,48,1920]{2,1,0:T(8,128)(2,1)S(1)}, bf16[1,48,1920]{2,1,0:T(8,128)(2,1)S(1)}, u32[]{:S(2)}, u32[]{:S(2)}) collective-permute-start(bf16[1,48,1920]{2,1,0:T(8,128)(2,1)S(1)} %fusion.30), channel_id=1, source_target_pairs={{0,2},{1,3},{2,0},{3,1},{4,6},{5,7},{6,4},{7,5},{8,10},{9,11},{10,... | collective-permute-start | bytes 552968 | tf_op jit(solution)/shard_map/ppermute | solution.py:670
  294.1 25.0 %collective-permute-start.34 = (bf16[8,48,1536]{2,1,0:T(8,128)(2,1)S(1)}, bf16[8,48,1536]{2,1,0:T(8,128)(2,1)S(1)}, u32[]{:S(2)}, u32[]{:S(2)}) collective-permute-start(bf16[8,48,1536]{2,1,0:T(8,128)(2,1)S(1)} %pad_maximum_fusion.7), channel_id=1, source_target_pairs={{0,8},{4,12},{8,0},{12,4},{16,24},{20,28},{24,16},{28,20},{1,9},{5... | collective-permute-start | bytes 3538952 | tf_op jit(solution)/shard_map/ppermute | solution.py:670
  301.2 16.7 %collective-permute-start.37 = (bf16[2,48,1920]{2,1,0:T(8,128)(2,1)S(1)}, bf16[2,48,1920]{2,1,0:T(8,128)(2,1)S(1)}, u32[]{:S(2)}, u32[]{:S(2)}) collective-permute-start(bf16[2,48,1920]{2,1,0:T(8,128)(2,1)S(1)} %pad_maximum_fusion.17), channel_id=1, source_target_pairs={{0,1},{1,0},{2,3},{3,2},{4,5},{5,4},{6,7},{7,6},{8,9},{9,8},{10,11... | collective-permute-start | bytes 1105928 | tf_op jit(solution)/shard_map/ppermute | solution.py:670
  301.3 19.4 %collective-permute-start.30 = (bf16[2,128,768]{2,1,0:T(8,128)(2,1)S(1)}, bf16[2,128,768]{2,1,0:T(8,128)(2,1)S(1)}, u32[]{:S(2)}, u32[]{:S(2)}) collective-permute-start(bf16[2,128,768]{2,1,0:T(8,128)(2,1)S(1)} %copy-done.31), channel_id=1, source_target_pairs={{0,2},{1,3},{2,0},{3,1},{4,6},{5,7},{6,4},{7,5},{8,10},{9,11},{10,... | collective-permute-start | bytes 1179656 | tf_op jit(solution)/shard_map/ppermute | solution.py:670
  318.2 5.3 %copy-start.30 = (bf16[2,128,768]{2,1,0:T(8,128)(2,1)S(1)}, bf16[2,128,768]{2,1,0:T(8,128)(2,1)}, u32[]{:S(2)}) copy-start(bf16[2,128,768]{2,1,0:T(8,128)(2,1)} %get-tuple-element.334) | copy-start | bytes 1179652
  320.7 17.6 %collective-permute-start.38 = (bf16[16,48,1536]{2,1,0:T(8,128)(2,1)}, bf16[16,48,1536]{2,1,0:T(8,128)(2,1)}, u32[]{:S(2)}, u32[]{:S(2)}) collective-permute-start(bf16[16,48,1536]{2,1,0:T(8,128)(2,1)} %pad_maximum_fusion.refs_0_), channel_id=1, source_target_pairs={{0,4},{4,0},{8,12},{12,8},{16,20},{20,16},{24,28},{28,24},{1,5},{5... | collective-permute-start | bytes 7077896 | tf_op jit(solution)/shard_map/ppermute | solution.py:670
  320.7 17.6 %collective-permute-start.39 = (bf16[16,48,1536]{2,1,0:T(8,128)(2,1)S(1)}, bf16[16,48,1536]{2,1,0:T(8,128)(2,1)}, u32[]{:S(2)}, u32[]{:S(2)}) collective-permute-start(bf16[16,48,1536]{2,1,0:T(8,128)(2,1)S(1)} %pad_maximum_fusion.1.refs_1_), channel_id=1, source_target_pairs={{0,4},{4,0},{8,12},{12,8},{16,20},{20,16},{24,28},{28,24},{1,5},{5... | collective-permute-start | bytes 7077896 | tf_op jit(solution)/shard_map/ppermute | solution.py:670
  321.2 10.0 %collective-permute-start.42 = (bf16[4,48,896]{2,1,0:T(8,128)(2,1)S(1)}, bf16[4,48,896]{2,1,0:T(8,128)(2,1)S(1)}, u32[]{:S(2)}, u32[]{:S(2)}) collective-permute-start(bf16[4,48,896]{2,1,0:T(8,128)(2,1)S(1)} %pad_maximum_fusion.18), channel_id=1, source_target_pairs={{0,8},{4,12},{8,0},{12,4},{16,24},{20,28},{24,16},{28,20},{1,9},{5... | collective-permute-start | bytes 1032200 | tf_op jit(solution)/shard_map/ppermute | solution.py:670
  321.9 10.8 %collective-permute-start.41 = (bf16[4,48,1024]{2,1,0:T(8,128)(2,1)S(1)}, bf16[4,48,1024]{2,1,0:T(8,128)(2,1)S(1)}, u32[]{:S(2)}, u32[]{:S(2)}) collective-permute-start(bf16[4,48,1024]{2,1,0:T(8,128)(2,1)S(1)} %fusion.15), channel_id=1, source_target_pairs={{0,16},{4,20},{8,24},{12,28},{16,0},{20,4},{24,8},{28,12},{1,17},{... | collective-permute-start | bytes 1179656 | tf_op jit(solution)/shard_map/ppermute | solution.py:670
  323.5 10.6 %collective-permute-start.40 = (bf16[2,128,768]{2,1,0:T(8,128)(2,1)S(1)}, bf16[2,128,768]{2,1,0:T(8,128)(2,1)}, u32[]{:S(2)}, u32[]{:S(2)}) collective-permute-start(bf16[2,128,768]{2,1,0:T(8,128)(2,1)S(1)} %copy-done.30), channel_id=1, source_target_pairs={{0,1},{1,0},{2,3},{3,2},{4,5},{5,4},{6,7},{7,6},{8,9},{9,8},{10,11... | collective-permute-start | bytes 1179656 | tf_op jit(solution)/shard_map/ppermute | solution.py:670
  334.1 18.1 %collective-permute-start.43 = (bf16[8,48,1024]{2,1,0:T(8,128)(2,1)S(1)}, bf16[8,48,1024]{2,1,0:T(8,128)(2,1)}, u32[]{:S(2)}, u32[]{:S(2)}) collective-permute-start(bf16[8,48,1024]{2,1,0:T(8,128)(2,1)S(1)} %pad_maximum_fusion.10), channel_id=1, source_target_pairs={{0,8},{4,12},{8,0},{12,4},{16,24},{20,28},{24,16},{28,20},{1,9},{5... | collective-permute-start | bytes 2359304 | tf_op jit(solution)/shard_map/ppermute | solution.py:670
  335.4 16.0 %collective-permute-start.44 = (bf16[8,48,896]{2,1,0:T(8,128)(2,1)}, bf16[8,48,896]{2,1,0:T(8,128)(2,1)}, u32[]{:S(2)}, u32[]{:S(2)}) collective-permute-start(bf16[8,48,896]{2,1,0:T(8,128)(2,1)} %pad_maximum_fusion.11), channel_id=1, source_target_pairs={{0,16},{4,20},{8,24},{12,28},{16,0},{20,4},{24,8},{28,12},{1,17},{... | collective-permute-start | bytes 2064392 | tf_op jit(solution)/shard_map/ppermute | solution.py:670
  335.9 13.8 %collective-permute-start.29 = (bf16[2,128,768]{2,1,0:T(8,128)(2,1)}, bf16[2,128,768]{2,1,0:T(8,128)(2,1)}, u32[]{:S(2)}, u32[]{:S(2)}) collective-permute-start(bf16[2,128,768]{2,1,0:T(8,128)(2,1)} %get-tuple-element.320), channel_id=1, source_target_pairs={{0,3},{1,2},{2,1},{3,0},{4,7},{5,6},{6,5},{7,4},{8,11},{9,10},{10,... | collective-permute-start | bytes 1179656 | tf_op jit(solution)/shard_map/ppermute | solution.py:670
  355.5 6.6 %collective-permute-start.45 = (bf16[16,48,1024]{2,1,0:T(8,128)(2,1)S(1)}, bf16[16,48,1024]{2,1,0:T(8,128)(2,1)}, u32[]{:S(2)}, u32[]{:S(2)}) collective-permute-start(bf16[16,48,1024]{2,1,0:T(8,128)(2,1)S(1)} %pad_maximum_fusion.5.refs_0_), channel_id=1, source_target_pairs={{0,4},{4,0},{8,12},{12,8},{16,20},{20,16},{24,28},{28,24},{1,5},{5... | collective-permute-start | bytes 4718600 | tf_op jit(solution)/shard_map/ppermute | solution.py:670
  355.6 5.4 %collective-permute-start.46 = (bf16[16,48,896]{2,1,0:T(8,128)(2,1)S(1)}, bf16[16,48,896]{2,1,0:T(8,128)(2,1)S(1)}, u32[]{:S(2)}, u32[]{:S(2)}) collective-permute-start(bf16[16,48,896]{2,1,0:T(8,128)(2,1)S(1)} %pad_maximum_fusion.6.refs_1_), channel_id=1, source_target_pairs={{0,4},{4,0},{8,12},{12,8},{16,20},{20,16},{24,28},{28,24},{1,5},{5... | collective-permute-start | bytes 4128776 | tf_op jit(solution)/shard_map/ppermute | solution.py:670
  (22 other events, 36.6 us)
